TPU v7x, 32 devices: a whole 2x2x4 slice. The times are simulated.
32 devices in a mesh: rows: 16 (over z, y, x), cols: 2 (over core).
Axes of the slice: x: 2, y: 2, z: 4, core: 2. Of those that a mesh axis runs over, the one named last changes fastest.
Arguments:
- queries: bfloat16 [8192, 128], P('rows'), may hold values from -1 to 1
- prototypes: bfloat16 [16384, 128], P('cols'), may hold values from -1 to 1
- potential: float32 [16384], P('cols'), may hold values from -0.15 to 0.15
- weights: int32 [8192], P('rows'), may hold values from 1 to 10, as said below
- capacity: int32 [16384], P('cols'), may hold values from 1 to 7, as said below
- cotangent: bfloat16 [8192, 128], P('rows'), may hold values from -16 to 16
Outputs:
- grad_queries: float32 [8192, 128], P(('rows', 'cols'))
- grad_protos: float32 [16384, 128], P('cols')
Inputs may be any that keep to these rules, and one draw needn't show every extreme that they name: weights rise along the queries: the first quarter are all 1, the k-th quarter (k = 0..3) lies in 1 + k to 1 + 3 k. `capacity`: capacities rise along the slots: the k-th quarter (k = 0..3) lies in 1 + k to 1 + 2 k.
All inputs are finite; a program needn't handle non-finite values.
Results may differ from a plain program's by a relative error of at most 0.0019.
The roundings to bfloat16 on the way count: a program that leaves them out, or rounds other values in their place, can miss the bound.
Values sent between devices are 32-bit elements; how exact they have to be, the bound alone decides.
A program may use at most 128 MiB of HBM per device.

v0:
```python
import math

import jax
import jax.numpy as jnp
from jax import lax
from jax.sharding import PartitionSpec as P

TEMPER = 0.05


def unit_rows(matrix):
    wide = matrix.astype(jnp.float32)
    length = jnp.sqrt(jnp.sum(wide * wide, axis=1) + 1e-06)
    return ((wide / length[:, None]).astype(jnp.bfloat16), length)


def unit_back(grad, unit, length):
    wide = unit.astype(jnp.float32)
    along = jnp.sum(wide * grad, axis=1, keepdims=True)
    return (grad - wide * along) / length[:, None]


def pair_dot(left, right):
    return lax.dot_general(
        left, right, (((1,), (1,)), ((), ())), preferred_element_type=jnp.float32
    )


def across_slots(stack):
    return lax.psum(stack, "cols")


def across_queries(stack):
    return lax.psum(stack, "rows")


def local(queries, prototypes, potential, weights, capacity, cotangent):
    qhat, qlen = unit_rows(queries)
    phat, plen = unit_rows(prototypes)
    wgt = weights.astype(jnp.float32)
    scaled = (cotangent.astype(jnp.float32) / wgt[:, None]).astype(jnp.bfloat16)
    local_rows = qhat.shape[0]
    slots = phat.shape[0]
    width = math.gcd(slots, 512)
    starts = list(range(0, slots, width))

    def kernel_tile(start):
        scores = pair_dot(qhat, phat[start : start + width])
        weight_cols = capacity[start : start + width].astype(jnp.float32)
        return weight_cols[None, :] * jnp.exp(
            (scores - potential[start : start + width][None, :]) / TEMPER
        )

    def coupling_tile(start):
        return pair_dot(scaled, phat[start : start + width])

    ztot = jnp.zeros((local_rows,), jnp.float32)
    kgsum = jnp.zeros((local_rows,), jnp.float32)
    for start in starts:
        kern = kernel_tile(start)
        ztot = ztot + jnp.sum(kern, axis=1)
        kgsum = kgsum + jnp.sum(kern * coupling_tile(start), axis=1)
    totals = across_slots(jnp.stack([ztot, kgsum]))
    share = wgt / totals[0]
    pvec = share * totals[1]
    alpha_one = pvec / wgt
    col_parts, q_parts, t_parts = ([], [], [])
    for start in starts:
        plan = share[:, None] * kernel_tile(start)
        col_parts.append(jnp.sum(plan, axis=0))
        q_parts.append(jnp.sum(plan * coupling_tile(start), axis=0))
    summed = across_queries(jnp.stack([jnp.concatenate(col_parts), jnp.concatenate(q_parts)]))
    colsum, qvec = (summed[0], summed[1])
    for start in starts:
        plan = share[:, None] * kernel_tile(start)
        t_parts.append(jnp.sum(alpha_one[:, None] * plan, axis=0))
    t_one = across_queries(jnp.concatenate(t_parts)[None, :])[0]
    beta_one = (qvec - t_one) / colsum
    rowprod = jnp.zeros((local_rows,), jnp.float32)
    for start in starts:
        plan = share[:, None] * kernel_tile(start)
        rowprod = rowprod + jnp.sum(plan * beta_one[start : start + width][None, :], axis=1)
    rowprod = across_slots(rowprod[None, :])[0]
    alpha_two = (pvec - rowprod) / wgt
    t_parts = []
    for start in starts:
        plan = share[:, None] * kernel_tile(start)
        t_parts.append(jnp.sum(alpha_two[:, None] * plan, axis=0))
    t_two = across_queries(jnp.concatenate(t_parts)[None, :])[0]
    beta_two = (qvec - t_two) / colsum
    dqhat = jnp.zeros(qhat.shape, jnp.float32)
    dp_parts = []
    for start in starts:
        plan = share[:, None] * kernel_tile(start)
        coupling = coupling_tile(start)
        shift_cols = beta_two[start : start + width][None, :]
        dscore = (plan * (coupling - alpha_two[:, None] - shift_cols) / TEMPER).astype(jnp.bfloat16)
        planb = plan.astype(jnp.bfloat16)
        dqhat = dqhat + jnp.dot(
            dscore, phat[start : start + width], preferred_element_type=jnp.float32
        )
        part = lax.dot_general(
            dscore, qhat, (((0,), (0,)), ((), ())), preferred_element_type=jnp.float32
        )
        part = part + lax.dot_general(
            planb, scaled, (((0,), (0,)), ((), ())), preferred_element_type=jnp.float32
        )
        dp_parts.append(part)
    dphat = jnp.concatenate(dp_parts, axis=0)
    query_part = lax.psum_scatter(dqhat, "cols", scatter_dimension=0, tiled=True)
    piece = query_part.shape[0]
    begin = lax.axis_index("cols") * piece
    grad_queries = unit_back(
        query_part,
        lax.dynamic_slice_in_dim(qhat, begin, piece, 0),
        lax.dynamic_slice_in_dim(qlen, begin, piece, 0),
    )
    whole = lax.psum(dphat, "rows")
    grad_protos = unit_back(whole, phat, plen)
    return (grad_queries, grad_protos)


def solution(mesh):
    in_specs = (P("rows", None), P("cols", None), P("cols"), P("rows"), P("cols"), P("rows", None))
    out_specs = (P(("rows", "cols"), None), P("cols", None))
    return jax.shard_map(local, mesh=mesh, in_specs=in_specs, out_specs=out_specs, check_vma=False)
```

profile of v0, /device:TPU:0, one launch (start us, length us, event | category | flops | bytes accessed | tf_op | source)
XLA Modules:
  0.0 491.0 jit_solution(12889176804840417390)
XLA Ops:
  8.1 2.7 fusion
  10.9 4.0 fusion.1
  21.2 1.5 fusion.156
  24.4 1.4 fusion.167
  25.9 1.5 fusion.166
  27.3 1.4 fusion.165
  28.8 1.4 fusion.164
  30.2 1.4 fusion.163
  31.7 1.5 fusion.162
  33.1 1.5 fusion.161
  34.6 1.5 fusion.160
  36.1 1.4 fusion.159
  37.5 1.5 fusion.158
  39.0 1.4 fusion.157
  40.5 1.5 fusion.155
  42.0 2.6 psum.42
  45.3 6.7 %multiply_reduce_fusion.95 = (f32[512]{0:T(512)S(1)}, f32[512]{0:T(512)S(1)}, f32[512]{0:T(512)S(1)}, f32[512]{0:T(512)S(1)}, f32[512]{0:T(512)S(1)}, /*index=5*...) fusion(f32[512,512]{1,0:T(8,128)} %get-tuple-element.254, ...), kind=kLoop, calls=%fused_computation.247 | loop fusion | flops 12570624 | bytes 16830464 | tf_op jit(solution)/shard_map/reduce_sum | solution.py:70
  55.0 3.3 multiply_reduce_fusion.94
  64.8 78.5 %psum.44 = f32[1,8192]{1,0:T(1,128)S(1)} all-reduce(f32[1,8192]{1,0:T(1,128)S(1)} %bitcast.105), channel_id=1, replica_groups=mesh['rows'=16,'cols'=2] {'rows'}, use_global_device_ids=true, to_apply=%region_84.0 | all-reduce | flops 8192 | bytes 65536 | tf_op jit(solution)/shard_map/psum | solution.py:34
  143.3 20.7 %all-reduce.3.cloned.1.call-done = f32[2,8192]{1,0:T(2,128)} async-done(((f32[2,8192]{1,0:T(2,128)}), f32[2,8192]{1,0:T(2,128)}) %all-reduce.3.cloned.1.call-update) | async-done | bytes 65552 | tf_op jit(solution)/shard_map/psum | solution.py:34
  165.1 4.1 multiply_reduce_fusion.31
  170.0 1.1 multiply_reduce_fusion.30
  171.2 2.5 psum.45
  174.3 6.3 %multiply_reduce_fusion = (f32[512]{0:T(512)S(1)}, f32[512]{0:T(512)S(1)}, f32[512]{0:T(512)S(1)}, f32[512]{0:T(512)S(1)}, f32[512]{0:T(512)S(1)}, /*index=5*/f3...) fusion(f32[512,512]{1,0:T(8,128)S(1)} %get-tuple-element.240, ...), kind=kLoop, calls=%fused_computation.136 | loop fusion | flops 12574720 | bytes 16814080 | tf_op jit(solution)/shard_map/reduce_sum | solution.py:88
  181.4 75.2 %psum.46 = f32[1,8192]{1,0:T(1,128)S(1)} all-reduce(f32[1,8192]{1,0:T(1,128)} %bitcast.104), channel_id=1, replica_groups=mesh['rows'=16,'cols'=2] {'rows'}, use_global_device_ids=true, to_apply=%region_118.0 | all-reduce | flops 8192 | bytes 65536 | tf_op jit(solution)/shard_map/psum | solution.py:34
  256.7 2.0 multiply_convert_fusion.15
  258.7 1.1 fusion.175
  259.7 1.2 fusion.150
  261.0 3.8 multiply_convert_fusion.1
  264.9 1.1 fusion.189
  266.0 1.1 fusion.180
  267.0 1.1 fusion.181
  270.3 1.2 multiply_convert_fusion
  271.5 1.1 fusion.176
  272.6 1.1 fusion.177
  273.6 1.1 fusion.178
  274.7 1.1 fusion.179
  275.8 1.2 multiply_convert_fusion.2
  277.0 1.0 fusion.188
  278.1 1.1 fusion.184
  279.1 1.1 fusion.185
  280.2 1.1 fusion.186
  281.2 1.1 fusion.187
  287.9 2.6 fusion.68
  290.4 2.6 fusion.67
  293.0 1.2 fusion.66
  294.2 1.2 fusion.65
  295.4 1.2 fusion.64
  296.6 1.2 fusion.63
  297.9 1.2 fusion.62
  299.1 1.2 fusion.61
  300.3 1.2 fusion.60
  301.5 1.2 fusion.59
  302.7 1.2 fusion.58
  303.9 1.2 fusion.57
  305.1 1.2 fusion.56
  306.3 1.2 fusion.55
  307.5 1.2 fusion.54
  309.0 1.2 fusion.53
  310.9 1.1 fusion.87
  312.0 1.7 fusion.89
  313.8 160.7 %all-reduce.5.cloned.1.call-done = f32[8192,128]{1,0:T(8,128)} async-done(((f32[8192,128]{1,0:T(8,128)}), f32[8192,128]{1,0:T(8,128)}) %all-reduce.5.cloned.1.call-update) | async-done | bytes 4194320 | tf_op jit(solution)/shard_map/psum | solution.py:118
  474.4 4.2 fusion.2
  478.6 5.6 %fusion.4 = f32[8192,128]{1,0:T(8,128)} fusion(f32[8192,128]{1,0:T(8,128)S(1)} %copy-done.42, f32[8192]{0:T(1024)S(1)} %fusion.2, f32[8192]{0:T(1024)S(1)} %add_sqrt_fusion, bf16[8192,128]{1,0:T(8,128)(2,1)S(1)} %copy-done.41), kind=kLoop, calls=%fused_computation.8 | loop fusion | flops 7340032 | bytes 10551296 | tf_op jit(solution)/shard_map/div | solution.py:20
  (331 shorter events, 30.6 us)
Async XLA Ops:
  7.2 156.9 %all-reduce.3.cloned.1.call-start = ((), (), s32[]{:S(2)}) async-start(), calls=%async_computation.1 | async-start | bytes 131072 | tf_op jit(solution)/shard_map/psum | solution.py:34
  14.9 25.5 %copy-start.38 = (bf16[8192,128]{1,0:T(8,128)(2,1)}, bf16[8192,128]{1,0:T(8,128)(2,1)S(1)}, u32[]{:S(2)}) copy-start(bf16[8192,128]{1,0:T(8,128)(2,1)S(1)} %fusion.1) | copy-start | bytes 6291460
  15.3 25.2 %copy-start.53 = (f32[512,512]{1,0:T(8,128)}, f32[512,512]{1,0:T(8,128)S(1)}, u32[]{:S(2)}) copy-start(f32[512,512]{1,0:T(8,128)S(1)} %fusion.147) | copy-start | bytes 3145732
  15.6 23.4 %copy-start.56 = (f32[512,512]{1,0:T(8,128)}, f32[512,512]{1,0:T(8,128)S(1)}, u32[]{:S(2)}) copy-start(f32[512,512]{1,0:T(8,128)S(1)} %fusion.143) | copy-start | bytes 3145732
  16.0 21.5 %copy-start.59 = (f32[512,512]{1,0:T(8,128)}, f32[512,512]{1,0:T(8,128)S(1)}, u32[]{:S(2)}) copy-start(f32[512,512]{1,0:T(8,128)S(1)} %fusion.139) | copy-start | bytes 3145732
  16.4 19.7 %copy-start.62 = (f32[512,512]{1,0:T(8,128)}, f32[512,512]{1,0:T(8,128)S(1)}, u32[]{:S(2)}) copy-start(f32[512,512]{1,0:T(8,128)S(1)} %fusion.135) | copy-start | bytes 3145732
  16.7 17.9 %copy-start.67 = (f32[512,512]{1,0:T(8,128)}, f32[512,512]{1,0:T(8,128)S(1)}, u32[]{:S(2)}) copy-start(f32[512,512]{1,0:T(8,128)S(1)} %fusion.131) | copy-start | bytes 3145732
  17.1 16.0 %copy-start.69 = (f32[512,512]{1,0:T(8,128)}, f32[512,512]{1,0:T(8,128)S(1)}, u32[]{:S(2)}) copy-start(f32[512,512]{1,0:T(8,128)S(1)} %fusion.127) | copy-start | bytes 3145732
  17.5 14.2 %copy-start.71 = (f32[512,512]{1,0:T(8,128)}, f32[512,512]{1,0:T(8,128)S(1)}, u32[]{:S(2)}) copy-start(f32[512,512]{1,0:T(8,128)S(1)} %fusion.123) | copy-start | bytes 3145732
  17.9 12.4 %copy-start.73 = (f32[512,512]{1,0:T(8,128)}, f32[512,512]{1,0:T(8,128)S(1)}, u32[]{:S(2)}) copy-start(f32[512,512]{1,0:T(8,128)S(1)} %fusion.119) | copy-start | bytes 3145732
  18.2 10.6 %copy-start.43 = (f32[512,512]{1,0:T(8,128)}, f32[512,512]{1,0:T(8,128)S(1)}, u32[]{:S(2)}) copy-start(f32[512,512]{1,0:T(8,128)S(1)} %fusion.115) | copy-start | bytes 3145732
  18.6 8.8 %copy-start.45 = (f32[512,512]{1,0:T(8,128)}, f32[512,512]{1,0:T(8,128)S(1)}, u32[]{:S(2)}) copy-start(f32[512,512]{1,0:T(8,128)S(1)} %fusion.111) | copy-start | bytes 3145732
  19.0 6.9 %copy-start.47 = (f32[512,512]{1,0:T(8,128)}, f32[512,512]{1,0:T(8,128)S(1)}, u32[]{:S(2)}) copy-start(f32[512,512]{1,0:T(8,128)S(1)} %fusion.107) | copy-start | bytes 3145732
  19.3 5.1 %copy-start.49 = (f32[512,512]{1,0:T(8,128)}, f32[512,512]{1,0:T(8,128)S(1)}, u32[]{:S(2)}) copy-start(f32[512,512]{1,0:T(8,128)S(1)} %fusion.103) | copy-start | bytes 3145732
  39.0 5.6 %copy-start.97 = (s32[512]{0:T(512)S(1)}, s32[512]{0:T(512)}, u32[]{:S(2)}) copy-start(s32[512]{0:T(512)} %param.9) | copy-start | bytes 6148
  45.2 6.8 %copy-start.13 = (f32[512,512]{1,0:T(8,128)S(1)}, f32[512,512]{1,0:T(8,128)}, u32[]{:S(2)}) copy-start(f32[512,512]{1,0:T(8,128)} %get-tuple-element.247) | copy-start | bytes 3145732
  45.2 6.8 %copy-start.17 = (f32[512,512]{1,0:T(8,128)S(1)}, f32[512,512]{1,0:T(8,128)}, u32[]{:S(2)}) copy-start(f32[512,512]{1,0:T(8,128)} %get-tuple-element.255) | copy-start | bytes 3145732
  45.2 6.8 %copy-start.20 = (f32[512,512]{1,0:T(8,128)S(1)}, f32[512,512]{1,0:T(8,128)}, u32[]{:S(2)}) copy-start(f32[512,512]{1,0:T(8,128)} %get-tuple-element.248) | copy-start | bytes 3145732
  45.2 6.8 %copy-start.23 = (f32[512,512]{1,0:T(8,128)S(1)}, f32[512,512]{1,0:T(8,128)}, u32[]{:S(2)}) copy-start(f32[512,512]{1,0:T(8,128)} %get-tuple-element.249) | copy-start | bytes 3145732
  45.2 6.9 %copy-start.26 = (f32[512,512]{1,0:T(8,128)S(1)}, f32[512,512]{1,0:T(8,128)}, u32[]{:S(2)}) copy-start(f32[512,512]{1,0:T(8,128)} %get-tuple-element.250) | copy-start | bytes 3145732
  45.2 6.9 %copy-start.29 = (f32[512,512]{1,0:T(8,128)S(1)}, f32[512,512]{1,0:T(8,128)}, u32[]{:S(2)}) copy-start(f32[512,512]{1,0:T(8,128)} %get-tuple-element.251) | copy-start | bytes 3145732
  45.2 7.0 %copy-start.32 = (f32[512,512]{1,0:T(8,128)S(1)}, f32[512,512]{1,0:T(8,128)}, u32[]{:S(2)}) copy-start(f32[512,512]{1,0:T(8,128)} %get-tuple-element.252) | copy-start | bytes 3145732
  45.2 7.3 %copy-start.35 = (f32[512,512]{1,0:T(8,128)S(1)}, f32[512,512]{1,0:T(8,128)}, u32[]{:S(2)}) copy-start(f32[512,512]{1,0:T(8,128)} %get-tuple-element.253) | copy-start | bytes 3145732
  45.2 7.6 %copy-start.54 = (f32[512,512]{1,0:T(8,128)S(1)}, f32[512,512]{1,0:T(8,128)}, u32[]{:S(2)}) copy-start(f32[512,512]{1,0:T(8,128)} %copy-done.53) | copy-start | bytes 3145732
  45.3 7.9 %copy-start.57 = (f32[512,512]{1,0:T(8,128)S(1)}, f32[512,512]{1,0:T(8,128)}, u32[]{:S(2)}) copy-start(f32[512,512]{1,0:T(8,128)} %copy-done.56) | copy-start | bytes 3145732
  45.3 8.2 %copy-start.60 = (f32[512,512]{1,0:T(8,128)S(1)}, f32[512,512]{1,0:T(8,128)}, u32[]{:S(2)}) copy-start(f32[512,512]{1,0:T(8,128)} %copy-done.59) | copy-start | bytes 3145732
  45.3 8.5 %copy-start.63 = (f32[512,512]{1,0:T(8,128)S(1)}, f32[512,512]{1,0:T(8,128)}, u32[]{:S(2)}) copy-start(f32[512,512]{1,0:T(8,128)} %copy-done.62) | copy-start | bytes 3145732
  45.3 8.8 %copy-start.68 = (f32[512,512]{1,0:T(8,128)S(1)}, f32[512,512]{1,0:T(8,128)}, u32[]{:S(2)}) copy-start(f32[512,512]{1,0:T(8,128)} %copy-done.67) | copy-start | bytes 3145732
  45.3 9.1 %copy-start.70 = (f32[512,512]{1,0:T(8,128)S(1)}, f32[512,512]{1,0:T(8,128)}, u32[]{:S(2)}) copy-start(f32[512,512]{1,0:T(8,128)} %copy-done.69) | copy-start | bytes 3145732
  45.3 9.4 %copy-start.72 = (f32[512,512]{1,0:T(8,128)S(1)}, f32[512,512]{1,0:T(8,128)}, u32[]{:S(2)}) copy-start(f32[512,512]{1,0:T(8,128)} %copy-done.71) | copy-start | bytes 3145732
  45.3 9.7 %copy-start.74 = (f32[512,512]{1,0:T(8,128)S(1)}, f32[512,512]{1,0:T(8,128)}, u32[]{:S(2)}) copy-start(f32[512,512]{1,0:T(8,128)} %copy-done.73) | copy-start | bytes 3145732
  59.3 251.6 %reduce-scatter.2.cloned.1.call-start = ((), (), s32[]{:S(2)}) async-start(), calls=%async_computation.2 | async-start | bytes 393216 | tf_op jit(solution)/shard_map/reduce_scatter | solution.py:110
  165.1 4.3 copy-start.10
  165.1 4.6 copy-start.14
  165.1 4.9 %copy-start.18 = (f32[512,512]{1,0:T(8,128)S(1)}, f32[512,512]{1,0:T(8,128)}, u32[]{:S(2)}) copy-start(f32[512,512]{1,0:T(8,128)} %get-tuple-element.255) | copy-start | bytes 3145732
  174.3 82.3 %copy-start.93 = (f32[2,8192]{1,0:T(2,128)S(1)}, f32[2,8192]{1,0:T(2,128)}, u32[]{:S(2)}) copy-start(f32[2,8192]{1,0:T(2,128)} %all-reduce.3.cloned.1.call-done) | copy-start | bytes 196612
  256.7 4.3 copy-start.15
  256.7 4.3 copy-start.21
  256.7 4.3 copy-start.24
  256.7 4.3 copy-start.27
  261.0 9.2 %copy-start.55 = (f32[512,512]{1,0:T(8,128)S(1)}, f32[512,512]{1,0:T(8,128)}, u32[]{:S(2)}) copy-start(f32[512,512]{1,0:T(8,128)} %copy-done.53) | copy-start | bytes 3145732
  261.0 9.2 %copy-start.58 = (f32[512,512]{1,0:T(8,128)S(1)}, f32[512,512]{1,0:T(8,128)}, u32[]{:S(2)}) copy-start(f32[512,512]{1,0:T(8,128)} %copy-done.56) | copy-start | bytes 3145732
  261.0 9.2 %copy-start.61 = (f32[512,512]{1,0:T(8,128)S(1)}, f32[512,512]{1,0:T(8,128)}, u32[]{:S(2)}) copy-start(f32[512,512]{1,0:T(8,128)} %copy-done.59) | copy-start | bytes 3145732
  261.0 9.2 %copy-start.64 = (f32[512,512]{1,0:T(8,128)S(1)}, f32[512,512]{1,0:T(8,128)}, u32[]{:S(2)}) copy-start(f32[512,512]{1,0:T(8,128)} %copy-done.62) | copy-start | bytes 3145732
  261.0 9.2 %copy-start.66 = (f32[512,512]{1,0:T(8,128)S(1)}, f32[512,512]{1,0:T(8,128)}, u32[]{:S(2)}) copy-start(f32[512,512]{1,0:T(8,128)} %copy-done.65) | copy-start | bytes 3145732
  264.9 5.3 %copy-start.19 = (f32[512,512]{1,0:T(8,128)S(1)}, f32[512,512]{1,0:T(8,128)}, u32[]{:S(2)}) copy-start(f32[512,512]{1,0:T(8,128)} %get-tuple-element.255) | copy-start | bytes 3145732
  264.9 5.3 %copy-start.30 = (f32[512,512]{1,0:T(8,128)S(1)}, f32[512,512]{1,0:T(8,128)}, u32[]{:S(2)}) copy-start(f32[512,512]{1,0:T(8,128)} %get-tuple-element.251) | copy-start | bytes 3145732
  264.9 5.3 %copy-start.33 = (f32[512,512]{1,0:T(8,128)S(1)}, f32[512,512]{1,0:T(8,128)}, u32[]{:S(2)}) copy-start(f32[512,512]{1,0:T(8,128)} %get-tuple-element.252) | copy-start | bytes 3145732
  264.9 5.3 %copy-start.36 = (f32[512,512]{1,0:T(8,128)S(1)}, f32[512,512]{1,0:T(8,128)}, u32[]{:S(2)}) copy-start(f32[512,512]{1,0:T(8,128)} %get-tuple-element.253) | copy-start | bytes 3145732
  270.2 5.5 %copy-start.11 = (f32[512,512]{1,0:T(8,128)S(1)}, f32[512,512]{1,0:T(8,128)}, u32[]{:S(2)}) copy-start(f32[512,512]{1,0:T(8,128)} %get-tuple-element.246) | copy-start | bytes 3145732
  270.2 5.5 %copy-start.44 = (f32[512,512]{1,0:T(8,128)S(1)}, f32[512,512]{1,0:T(8,128)}, u32[]{:S(2)}) copy-start(f32[512,512]{1,0:T(8,128)} %copy-done.43) | copy-start | bytes 3145732
  270.2 5.5 %copy-start.46 = (f32[512,512]{1,0:T(8,128)S(1)}, f32[512,512]{1,0:T(8,128)}, u32[]{:S(2)}) copy-start(f32[512,512]{1,0:T(8,128)} %copy-done.45) | copy-start | bytes 3145732
  270.2 5.5 %copy-start.48 = (f32[512,512]{1,0:T(8,128)S(1)}, f32[512,512]{1,0:T(8,128)}, u32[]{:S(2)}) copy-start(f32[512,512]{1,0:T(8,128)} %copy-done.47) | copy-start | bytes 3145732
  270.2 5.5 %copy-start.50 = (f32[512,512]{1,0:T(8,128)S(1)}, f32[512,512]{1,0:T(8,128)}, u32[]{:S(2)}) copy-start(f32[512,512]{1,0:T(8,128)} %copy-done.49) | copy-start | bytes 3145732
  270.3 5.5 %copy-start.52 = (f32[512,512]{1,0:T(8,128)S(1)}, f32[512,512]{1,0:T(8,128)}, u32[]{:S(2)}) copy-start(f32[512,512]{1,0:T(8,128)} %copy-done.51) | copy-start | bytes 3145732
  271.5 15.0 %copy-start.77 = (bf16[512,512]{1,0:T(8,128)(2,1)}, bf16[512,512]{1,0:T(8,128)(2,1)S(1)}, u32[]{:S(2)}) copy-start(bf16[512,512]{1,0:T(8,128)(2,1)S(1)} %get-tuple-element.223) | copy-start | bytes 1572868
  271.5 4.3 copy-start.2
  271.5 4.3 copy-start.5
  271.5 4.3 copy-start.8
  277.0 5.3 %copy-start.39 = (bf16[8192,128]{1,0:T(8,128)(2,1)S(1)}, bf16[8192,128]{1,0:T(8,128)(2,1)}, u32[]{:S(2)}) copy-start(bf16[8192,128]{1,0:T(8,128)(2,1)} %copy-done.38) | copy-start | bytes 6291460
  287.5 186.9 %all-reduce.5.cloned.1.call-start = ((), (), s32[]{:S(2)}) async-start(), calls=%async_computation.3 | async-start | bytes 8388608 | tf_op jit(solution)/shard_map/psum | solution.py:118
  287.8 5.2 %copy-start.37 = (f32[512,512]{1,0:T(8,128)S(1)}, f32[512,512]{1,0:T(8,128)}, u32[]{:S(2)}) copy-start(f32[512,512]{1,0:T(8,128)} %get-tuple-element.253) | copy-start | bytes 3145732
  287.8 5.2 %copy-start.91 = (f32[512,128]{1,0:T(8,128)S(1)}, f32[512,128]{1,0:T(8,128)}, u32[]{:S(2)}) copy-start(f32[512,128]{1,0:T(8,128)} %fusion.177) | copy-start | bytes 786436
  310.2 164.2 %copy-start.41 = (bf16[8192,128]{1,0:T(8,128)(2,1)S(1)}, bf16[8192,128]{1,0:T(8,128)(2,1)}, u32[]{:S(2)}) copy-start(bf16[8192,128]{1,0:T(8,128)(2,1)} %param.7) | copy-start | bytes 6291460
  (39 other events, 101.5 us)
Sparse Core Ops, SparseCore 0:
  59.4 104.5 all-reduce.2
  287.7 3.5 reduce-scatter.1
  310.3 164.0 all-reduce.4
where the time goes:
time: 494 us; the launch traced here: 491 us
  waiting for transfers between devices  181 us (37%)
  blocking collectives  159 us (32%)
  matrix products  70.6 us (14%)
  other arithmetic  53.2 us (11%)
  between operations  15.6 us (3%)
  local copies, waits for them, and re-layouts  11.1 us (2%)
    psum x1, waiting for transfers between devices, local(): whole = lax.psum(dphat, 'rows')  161 us
    psum x2, blocking collectives, across_queries(): return lax.psum(stack, 'rows')  154 us
    dot_general x32, matrix products, pair_dot(): lax.dot_general(left, right, (((1,), (1,)), ((), ())), preferred_element_...  26.3 us
    dot_general x16, matrix products, local(): lax.dot_general(planb, scaled, (((0,), (0,)), ((), ())), preferred_elemen...  21.8 us
    psum x1, waiting for transfers between devices, across_queries(): return lax.psum(stack, 'rows')  20.7 us
    dot_general x16, matrix products, local(): lax.dot_general(dscore, qhat, (((0,), (0,)), ((), ())), preferred_element...  16.2 us
    unnamed x259, local copies, waits for them, and re-layouts  10.9 us
    reduce_sum x2, other arithmetic, local(): col_parts.append(jnp.sum(plan, axis=0))  9.92 us
  transfers between devices with their start and end apart: 3, of which 2 were waited for; matrix products, arithmetic and copies ran while one was open for 6% of the time, Pallas kernels for 0%

commit v1 on v0

v1 whole, which is shorter than its diff:
```python
import functools
import math

import jax
import jax.numpy as jnp
from jax import lax
from jax.experimental import pallas as pl
from jax.experimental.pallas import tpu as pltpu
from jax.sharding import PartitionSpec as P

TEMPER = 0.05
LANES = 128
MESH = pl.DeviceIdType.MESH


def unit_rows(matrix):
    wide = matrix.astype(jnp.float32)
    length = jnp.sqrt(jnp.sum(wide * wide, axis=1) + 1e-06)
    return ((wide / length[:, None]).astype(jnp.bfloat16), length)


def unit_back(grad, unit, length):
    wide = unit.astype(jnp.float32)
    along = jnp.sum(wide * grad, axis=1, keepdims=True)
    return (grad - wide * along) / length[:, None]


def nt_dot(left, right):
    return lax.dot_general(
        left, right, (((1,), (1,)), ((), ())), preferred_element_type=jnp.float32
    )


def tiles_of(slots, rows):
    width = max(slots // rows, LANES)
    return width, slots // width


def push(src, dst, send, recv, device):
    return pltpu.make_async_remote_copy(
        src_ref=src, dst_ref=dst, send_sem=send, recv_sem=recv,
        device_id=device, device_id_type=MESH,
    )


def main_kernel(
    rows, cols, qhat, scaled, phat, offset, wgt, left_t, dp_out, dq_out,
    kern, coup, zacc, kacc, share, alpha, cbuf, part, pbuf, beta, gpart, gbuf, shift,
    invs, dqacc, dqbuf,
    csend, crecv, psend, precv, bsend, brecv, rsend, rrecv, gsend, grecv, hsend, hrecv,
    dsend, drecv,
):
    tiles, queries, width = kern.shape
    lanes = [slice(k, k + LANES) for k in range(0, width, LANES)]
    r = lax.axis_index("rows")
    c = lax.axis_index("cols")

    barrier = pltpu.get_barrier_semaphore()
    for o in range(1, rows):
        pl.semaphore_signal(
            barrier, inc=1, device_id=(lax.rem(r + o, rows), c), device_id_type=MESH
        )
    for o in range(1, cols):
        pl.semaphore_signal(
            barrier, inc=1, device_id=(r, lax.rem(c + o, cols)), device_id_type=MESH
        )

    zacc[...] = jnp.zeros_like(zacc)
    kacc[...] = jnp.zeros_like(kacc)
    dqacc[...] = jnp.zeros_like(dqacc)
    log2e = 1.0 / (TEMPER * math.log(2.0))
    step = min(queries, 256)

    def first(t, carry):
        proto = phat[t]
        base = offset[t]
        for q in range(0, queries, step):
            qs = slice(q, q + step)
            k = jnp.exp2(nt_dot(qhat[qs], proto) * log2e + base)
            g = nt_dot(scaled[qs], proto)
            kern[t, qs, :] = k
            coup[t, qs, :] = g
            kg = k * g
            zsum = k[:, lanes[0]]
            gsum = kg[:, lanes[0]]
            for l in lanes[1:]:
                zsum = zsum + k[:, l]
                gsum = gsum + kg[:, l]
            zacc[qs, :] += zsum
            kacc[qs, :] += gsum
        return carry

    lax.fori_loop(0, tiles, first, 0)
    pl.semaphore_wait(barrier, rows - 1 + cols - 1)

    lane = lax.broadcasted_iota(jnp.int32, (queries, LANES), 1)

    def over_cols(send, recv):
        copies = []
        for o in range(1, cols):
            cp = push(
                cbuf.at[0], cbuf.at[o], send.at[o], recv.at[o],
                (r, lax.rem(c + o, cols)),
            )
            cp.start()
            copies.append(cp)
        for cp in copies:
            cp.wait()
        total = cbuf[0]
        for o in range(1, cols):
            total = total + cbuf[o]
        return total

    ztot = jnp.sum(zacc[...], axis=1, keepdims=True)
    kgsum = jnp.sum(kacc[...], axis=1, keepdims=True)
    cbuf[0] = jnp.where(lane == 0, ztot, kgsum)
    total = over_cols(csend, crecv)
    ztot = total[:, 0:1]
    kgsum = total[:, 1:2]
    w = wgt[...]
    srate = w / ztot
    share[...] = jnp.broadcast_to(srate, share.shape)
    alpha[...] = jnp.broadcast_to(srate * kgsum / w, alpha.shape)

    def second(t, carry):
        for l in lanes:
            p = share[...] * kern[t, :, l]
            kern[t, :, l] = p
            part[t, 0:1, l] = jnp.sum(p, axis=0, keepdims=True)
            part[t, 1:2, l] = jnp.sum(
                p * (coup[t, :, l] - alpha[...]), axis=0, keepdims=True
            )
        return carry

    lax.fori_loop(0, tiles, second, 0)

    def scatter(src, dst, send, recv):
        def each(o, carry):
            peer = lax.rem(r + o, rows)

            def go():
                push(src.at[peer], dst.at[o], send.at[o], recv.at[o], (peer, c)).start()

            if tiles == rows:
                go()
            else:
                pl.when(peer < tiles)(go)
            return carry

        lax.fori_loop(1, rows, each, 0)

        def done(o, carry):
            peer = lax.rem(r + o, rows)

            def sent():
                push(src.at[0], dst.at[o], send.at[o], recv.at[o], (peer, c)).wait_send()

            def got():
                push(src.at[0], dst.at[o], send.at[o], recv.at[o], (peer, c)).wait_recv()

            if tiles == rows:
                sent()
                got()
            else:
                pl.when(peer < tiles)(sent)
                pl.when(r < tiles)(got)
            return carry

        lax.fori_loop(1, rows, done, 0)

    def spread(buf, send, recv):
        def each(o, carry):
            peer = lax.rem(r + o, rows)

            def go():
                push(buf.at[r], buf.at[r], send.at[o], recv.at[o], (peer, c)).start()

            if tiles == rows:
                go()
            else:
                pl.when(r < tiles)(go)
            return carry

        lax.fori_loop(1, rows, each, 0)

        def done(o, carry):
            origin = lax.rem(r + rows - o, rows)
            peer = lax.rem(r + o, rows)

            def sent():
                push(buf.at[r], buf.at[r], send.at[o], recv.at[o], (peer, c)).wait_send()

            def got():
                push(
                    buf.at[origin], buf.at[origin], send.at[o], recv.at[o], (peer, c)
                ).wait_recv()

            if tiles == rows:
                sent()
                got()
            else:
                pl.when(r < tiles)(sent)
                pl.when(origin < tiles)(got)
            return carry

        lax.fori_loop(1, rows, done, 0)

    def own(body):
        if tiles == rows:
            body()
        else:
            pl.when(r < tiles)(body)

    scatter(part, pbuf, psend, precv)

    def first_beta():
        both = part[r]
        for o in range(1, rows):
            both = both + pbuf[o]
        inv = 1.0 / both[0:1]
        invs[...] = inv
        beta[r] = both[1:2] * inv

    own(first_beta)
    spread(beta, bsend, brecv)

    zacc[...] = jnp.zeros_like(zacc)

    def third(t, carry):
        acc = zacc[...]
        for l in lanes:
            acc = acc + kern[t, :, l] * beta[t, :, l]
        zacc[...] = acc
        return carry

    lax.fori_loop(0, tiles, third, 0)
    rowprod = jnp.sum(zacc[...], axis=1, keepdims=True)
    cbuf2 = jnp.broadcast_to(rowprod, (queries, LANES))
    kacc[...] = cbuf2
    copies = []
    for o in range(1, cols):
        cp = push(
            kacc, dqbuf.at[o], rsend.at[o], rrecv.at[o], (r, lax.rem(c + o, cols))
        )
        cp.start()
        copies.append(cp)
    for cp in copies:
        cp.wait()
    rowtot = kacc[...]
    for o in range(1, cols):
        rowtot = rowtot + dqbuf[o]
    change = rowtot / w
    share[...] = change
    alpha[...] = alpha[...] - change

    def fourth(t, carry):
        for l in lanes:
            gpart[t, :, l] = jnp.sum(share[...] * kern[t, :, l], axis=0, keepdims=True)
        return carry

    lax.fori_loop(0, tiles, fourth, 0)
    scatter(gpart, gbuf, gsend, grecv)

    def second_beta():
        tot = gpart[r]
        for o in range(1, rows):
            tot = tot + gbuf[o]
        shift[r] = beta[r] + tot * invs[...]

    own(second_beta)
    spread(shift, hsend, hrecv)

    def fifth(t, carry):
        ds = []
        pb = []
        for l in lanes:
            p = kern[t, :, l]
            ds.append(
                (p * ((coup[t, :, l] - alpha[...]) - shift[t, :, l]) * (1.0 / TEMPER)).astype(
                    jnp.bfloat16
                )
            )
            pb.append(p.astype(jnp.bfloat16))
        ds = jnp.concatenate(ds, axis=1)
        pb = jnp.concatenate(pb, axis=1)
        dqacc[...] += jnp.dot(ds, phat[t], preferred_element_type=jnp.float32)
        dp_out[t] = jnp.dot(
            left_t[0], ds, preferred_element_type=jnp.float32
        ) + jnp.dot(left_t[1], pb, preferred_element_type=jnp.float32)
        return carry

    lax.fori_loop(0, tiles, fifth, 0)

    piece = queries // cols
    copies = []
    for o in range(1, cols):
        peer = lax.rem(c + o, cols)
        cp = push(
            dqacc.at[pl.ds(pl.multiple_of(peer * piece, 8), piece)],
            cbuf.at[o, pl.ds(0, piece)], dsend.at[o], drecv.at[o], (r, peer),
        )
        cp.start()
        copies.append(cp)
    for cp in copies:
        cp.wait()
    mine = dqacc[pl.ds(pl.multiple_of(c * piece, 8), piece), :]
    for o in range(1, cols):
        mine = mine + cbuf[o, 0:piece]
    dq_out[...] = mine


def run_main(rows, cols, qhat, scaled, phat, offset, wgt, left_t):
    queries, feats = qhat.shape
    tiles, width, _ = phat.shape
    f32 = jnp.float32
    vec = lambda *s: pltpu.VMEM(s, f32)
    sems_r = [pltpu.SemaphoreType.DMA((rows,))] * 2
    sems_c = [pltpu.SemaphoreType.DMA((cols,))] * 2
    return pl.pallas_call(
        functools.partial(main_kernel, rows, cols),
        out_shape=(
            jax.ShapeDtypeStruct((tiles, feats, width), f32),
            jax.ShapeDtypeStruct((queries // cols, feats), f32),
        ),
        in_specs=[pl.BlockSpec(memory_space=pltpu.VMEM)] * 6,
        out_specs=(pl.BlockSpec(memory_space=pltpu.VMEM),) * 2,
        scratch_shapes=[
            vec(tiles, queries, width), vec(tiles, queries, width),
            vec(queries, LANES), vec(queries, LANES), vec(queries, LANES), vec(queries, LANES),
            vec(cols, queries, LANES),
            vec(tiles, 2, width), vec(rows, 2, width), vec(tiles, 1, width),
            vec(tiles, 1, width), vec(rows, 1, width), vec(tiles, 1, width),
            vec(1, width), vec(queries, feats), vec(cols, queries, LANES),
        ]
        + sems_c + sems_r + sems_r + sems_c + sems_r + sems_r + sems_c,
        compiler_params=pltpu.CompilerParams(
            collective_id=0, has_side_effects=True, vmem_limit_bytes=56 * 1024 * 1024
        ),
        name="transport_sweeps",
    )(qhat, scaled, phat, offset, wgt, left_t)


def local(rows, cols, queries, prototypes, potential, weights, capacity, cotangent):
    qhat, qlen = unit_rows(queries)
    phat, plen = unit_rows(prototypes)
    wgt = weights.astype(jnp.float32)
    scaled = (cotangent.astype(jnp.float32) / wgt[:, None]).astype(jnp.bfloat16)
    slots, feats = phat.shape
    width, tiles = tiles_of(slots, rows)
    offset = jnp.log2(capacity.astype(jnp.float32)) - potential * (1.0 / (TEMPER * math.log(2.0)))
    dp, dq = run_main(
        rows, cols, qhat, scaled, phat.reshape(tiles, width, feats),
        offset.reshape(tiles, 1, width),
        jnp.broadcast_to(wgt[:, None], (wgt.shape[0], LANES))[:, :1],
        jnp.stack([qhat.T, scaled.T]),
    )
    piece = dq.shape[0]
    begin = lax.axis_index("cols") * piece
    grad_queries = unit_back(
        dq,
        lax.dynamic_slice_in_dim(qhat, begin, piece, 0),
        lax.dynamic_slice_in_dim(qlen, begin, piece, 0),
    )
    whole = lax.psum(dp, "rows")
    whole = whole.transpose(0, 2, 1).reshape(slots, feats)
    grad_protos = unit_back(whole, phat, plen)
    return (grad_queries, grad_protos)


def solution(mesh):
    rows, cols = mesh.shape["rows"], mesh.shape["cols"]
    in_specs = (P("rows", None), P("cols", None), P("cols"), P("rows"), P("cols"), P("rows", None))
    out_specs = (P(("rows", "cols"), None), P("cols", None))
    return jax.shard_map(
        functools.partial(local, rows, cols),
        mesh=mesh, in_specs=in_specs, out_specs=out_specs, check_vma=False,
    )
```

time: 494 us -> 265 us (0.54)
  blocking collectives: 159 us -> 0 us
  matrix products: 70.6 us -> 0 us
  Pallas kernels: 0 us -> 53.3 us
  other arithmetic: 53.2 us -> 19.2 us
  waiting for transfers between devices: 181 us -> 167 us
    psum x4 -> x0, blocking collectives: 159 us -> none  [the longest x2 154 us: across_queries(): return lax.psum(stack, 'rows')]
    dot_general x80 -> x0, matrix products: 70.6 us -> none  [the longest x32 26.3 us: pair_dot(): lax.dot_general(left, right, (((1,), (1,)), ((), ())), preferred_element_...]
    pallas_call x0 -> x1, Pallas kernels: none -> 53.3 us  [run_main(): pl.pallas_call(functools.partial(main_kernel, rows, cols), out_shape=(jax...]
    reduce_sum x5 -> x0, other arithmetic: 21.5 us -> none  [the longest x2 9.92 us: local(): col_parts.append(jnp.sum(plan, axis=0))]
    psum x2 -> x1, waiting for transfers between devices: 181 us -> 167 us  [local(): whole = lax.psum(dp, 'rows')]
    convert_element_type x5 -> x1, other arithmetic: 8.18 us -> 0.03 us  [local(): scaled = (cotangent.astype(jnp.float32) / wgt[:, None]).astype(jnp.bfloat16)]
    unnamed x259 -> x13, local copies, waits for them, and re-layouts: 10.9 us -> 3.81 us
    transpose x0 -> x1, local copies, waits for them, and re-layouts: none -> 5.32 us  [local(): whole = whole.transpose(0, 2, 1).reshape(slots, feats)]
  transfers between devices with their start and end apart: 3 -> 1, of which waited for: 2 -> 1; matrix products, arithmetic and copies ran while one was open for 6% -> 0% of each run, Pallas kernels for 0% -> 0%
where the time goes in v1:
time: 265 us
  waiting for transfers between devices  167 us (63%)
  Pallas kernels  53.3 us (20%)
  other arithmetic  19.2 us (7%)
  between operations  14.2 us (5%)
  local copies, waits for them, and re-layouts  11.7 us (4%)
    psum x1, waiting for transfers between devices, local(): whole = lax.psum(dp, 'rows')  167 us
    pallas_call x1, Pallas kernels, run_main(): pl.pallas_call(functools.partial(main_kernel, rows, cols), out_shape=(jax...  53.3 us
    div x2, other arithmetic, unit_back(): return (grad - wide * along) / length[:, None]  5.62 us
    transpose x1, local copies, waits for them, and re-layouts, local(): whole = whole.transpose(0, 2, 1).reshape(slots, feats)  5.32 us
  transfers between devices with their start and end apart: 1, of which 1 were waited for; matrix products, arithmetic and copies ran while one was open for 0% of the time, Pallas kernels for 0%

profile of v1, /device:TPU:0, one launch (start us, length us, event | category | flops | bytes accessed | tf_op | source)
XLA Modules:
  0.0 265.0 jit_solution(15441525782651485448)
XLA Ops:
  7.2 0.0 copy-start
  7.2 0.0 all-reduce.2.cloned.1.call-start
  7.2 1.1 copy.16
  8.4 0.7 convert_element_type.33
  9.1 0.0 copy-start.3
  9.1 0.0 copy-start.4
  9.2 1.0 copy.15
  10.3 0.8 copy.17.qhat
  11.1 0.8 copy.18.scaled
  11.8 2.7 %fusion = f32[8192]{0:T(1024)S(1)} fusion(bf16[8192,128]{1,0:T(8,128)(2,1)} %param.7), kind=kLoop, calls=%fused_computation.4 | loop fusion | flops 3137536 | bytes 2129920 | tf_op jit(solution)/shard_map/reduce_sum | solution.py:18
  14.6 0.0 copy-done
  14.6 4.4 %fusion.1 = bf16[8192,128]{1,0:T(8,128)(2,1)} fusion(bf16[8192,128]{1,0:T(8,128)(2,1)S(1)} %copy-done, f32[8192]{0:T(1024)S(1)} %add_sqrt_fusion), kind=kLoop, calls=%fused_computation.5 | loop fusion | flops 3145728 | bytes 4227072 | tf_op jit(solution)/shard_map/convert_element_type | solution.py:19
  19.0 0.8 copy.19.wgt
  19.8 0.0 copy-done.3
  19.8 0.0 copy-done.4
  19.8 0.6 multiply_subtract_fusion
  20.4 0.7 pad_maximum_fusion.left_t
  21.1 53.3 %transport_sweeps.1 = (f32[16,128,512]{2,1,0:T(8,128)}, f32[256,128]{1,0:T(8,128)}) custom-call(bf16[512,128]{1,0:T(8,128)(2,1)} %copy.17.qhat, bf16[512,128]{1,0:T(8,128)(2,1)} %copy.18.scaled, bf16[16,512,128]{2,1,0:T(8,128)(2,1)} %bitcast.14, f32[16,1,512]{2,1,0:T(1,128)} %bitcast.16, f32[512,1]{1,0:T(8,128)} %copy.19.wgt, ...), custom_call_target="tpu_custom_call" | custom-call | tf_op jit(solution)/shard_map/transport_sweeps/pallas_call | solution.py:319
  74.4 5.3 %copy.22 = f32[16,512,128]{2,1,0:T(8,128)} copy(f32[16,512,128]{1,2,0:T(8,128)} %bitcast.15) | data formatting | bytes 8388608 | tf_op jit(solution)/shard_map/transpose | solution.py:365
  79.8 0.0 copy-start.2
  79.8 0.0 all-reduce.2.cloned.1.call-update
  79.8 0.9 copy-done.2
  80.7 0.1 copy.21
  80.8 0.1 dynamic_slice.7
  80.9 0.8 copy.23
  81.7 166.7 %all-reduce.2.cloned.1.call-done = f32[8192,128]{1,0:T(8,128)} async-done(((f32[8192,128]{1,0:T(8,128)}), f32[8192,128]{1,0:T(8,128)}) %all-reduce.2.cloned.1.call-update) | async-done | bytes 4194320 | tf_op jit(solution)/shard_map/psum | solution.py:364
  248.3 0.0 copy-start.1
  248.3 4.2 %fusion.2 = f32[8192]{0:T(1024)S(1)} fusion(f32[8192,128]{1,0:T(8,128)} %all-reduce.2.cloned.1.call-done, f32[8192]{0:T(1024)S(1)} %add_sqrt_fusion, bf16[8192,128]{1,0:T(8,128)(2,1)S(1)} %copy-done), kind=kLoop, calls=%fused_computation.6 | loop fusion | flops 6283264 | bytes 6356992 | tf_op jit(solution)/shard_map/reduce_sum | solution.py:24
  252.5 0.0 copy-done.1
  252.6 5.6 %fusion.4 = f32[8192,128]{1,0:T(8,128)} fusion(f32[8192,128]{1,0:T(8,128)S(1)} %copy-done.1, f32[8192]{0:T(1024)S(1)} %fusion.2, f32[8192]{0:T(1024)S(1)} %add_sqrt_fusion, bf16[8192,128]{1,0:T(8,128)(2,1)S(1)} %copy-done), kind=kLoop, calls=%fused_computation.8 | loop fusion | flops 7340032 | bytes 10551296 | tf_op jit(solution)/shard_map/div | solution.py:25
  (9 shorter events, 0.3 us)
Async XLA Ops:
  7.2 7.4 %copy-start = (bf16[8192,128]{1,0:T(8,128)(2,1)S(1)}, bf16[8192,128]{1,0:T(8,128)(2,1)}, u32[]{:S(2)}) copy-start(bf16[8192,128]{1,0:T(8,128)(2,1)} %param.7) | copy-start | bytes 6291460
  7.2 241.2 %all-reduce.2.cloned.1.call-start = ((), (), s32[]{:S(2)}) async-start(), calls=%async_computation | async-start | bytes 8388608 | tf_op jit(solution)/shard_map/psum | solution.py:364
  9.1 10.7 %copy-start.3 = (f32[8192]{0:T(1024)S(1)}, f32[8192]{0:T(1024)}, u32[]{:S(2)}) copy-start(f32[8192]{0:T(1024)} %param.8) | copy-start | bytes 98308
  9.1 10.7 %copy-start.4 = (s32[8192]{0:T(1024)S(1)}, s32[8192]{0:T(1024)}, u32[]{:S(2)}) copy-start(s32[8192]{0:T(1024)} %param.10) | copy-start | bytes 98308
  79.8 0.9 copy-start.2
  248.3 4.2 %copy-start.1 = (f32[8192,128]{1,0:T(8,128)S(1)}, f32[8192,128]{1,0:T(8,128)}, u32[]{:S(2)}) copy-start(f32[8192,128]{1,0:T(8,128)} %all-reduce.2.cloned.1.call-done) | copy-start | bytes 12582916
Sparse Core Ops, SparseCore 0:
  79.9 168.4 all-reduce.1

commit v2 on v1

--- a/solution.py
+++ b/solution.py
@@ -44,11 +44,11 @@
 
 
 def main_kernel(
-    rows, cols, qhat, scaled, phat, offset, wgt, left_t, dp_out, dq_out,
+    rows, cols, fused, qhat, scaled, phat, offset, wgt, left_t, plen, dp_out, dq_out,
     kern, coup, zacc, kacc, share, alpha, cbuf, part, pbuf, beta, gpart, gbuf, shift,
     invs, dqacc, dqbuf,
     csend, crecv, psend, precv, bsend, brecv, rsend, rrecv, gsend, grecv, hsend, hrecv,
-    dsend, drecv,
+    dsend, drecv, *ring,
 ):
     tiles, queries, width = kern.shape
     lanes = [slice(k, k + LANES) for k in range(0, width, LANES)]
@@ -270,7 +270,12 @@
     own(second_beta)
     spread(shift, hsend, hrecv)
 
-    def fifth(t, carry):
+    if fused:
+        dp, rs1, rs2, rs3, s1s, s1r, s2s, s2r, s3s, s3r, as_, ar, bs, br, zs, zr = ring
+    else:
+        dp = dp_out
+
+    def fifth(t):
         ds = []
         pb = []
         for l in lanes:
@@ -284,12 +289,58 @@
         ds = jnp.concatenate(ds, axis=1)
         pb = jnp.concatenate(pb, axis=1)
         dqacc[...] += jnp.dot(ds, phat[t], preferred_element_type=jnp.float32)
-        dp_out[t] = jnp.dot(
+        dp[t] = jnp.dot(
             left_t[0], ds, preferred_element_type=jnp.float32
         ) + jnp.dot(left_t[1], pb, preferred_element_type=jnp.float32)
-        return carry
-
-    lax.fori_loop(0, tiles, fifth, 0)
+
+    if not fused:
+
+        def plain(t, carry):
+            fifth(t)
+            return carry
+
+        lax.fori_loop(0, tiles, plain, 0)
+    else:
+        depth = rows // 4
+        z = r // 4
+        even = lax.rem(c, 2) == 0
+        wa = jnp.where(even, 1, 2)
+        wb = 3 - wa
+        a = jnp.where(even, lax.rem(r, 2), lax.rem(r // 2, 2))
+        b = jnp.where(even, lax.rem(r // 2, 2), lax.rem(r, 2))
+        peer_a = r + (1 - 2 * a) * wa
+        peer_b = r + (1 - 2 * b) * wb
+
+        def spot(zz, av, bv):
+            return zz * 4 + av * wa + bv * wb
+
+        def ahead(k):
+            return lax.rem(z + 1 + k, depth)
+
+        def copy_a1(i, t):
+            return push(dp.at[t], rs1.at[i], s1s.at[i], s1r.at[i], (peer_a, c))
+
+        def copy_b1(k, t):
+            return push(dp.at[t], rs2.at[k], s2s.at[k], s2r.at[k], (peer_b, c))
+
+        def copy_z1(k, t):
+            return push(dp.at[t], rs3.at[k], s3s.at[k], s3r.at[k], (spot(ahead(k), a, b), c))
+
+        def leave(i, carry):
+            far = i < depth
+            t = spot(ahead(lax.rem(i, depth)), 1 - a, jnp.where(far, 1 - b, b))
+            fifth(t)
+            copy_a1(i, t).start()
+            return carry
+
+        lax.fori_loop(0, 2 * depth, leave, 0)
+
+        def stay(i, carry):
+            far = i < depth
+            fifth(spot(ahead(lax.rem(i, depth)), a, jnp.where(far, 1 - b, b)))
+            return carry
+
+        lax.fori_loop(0, 2 * depth, stay, 0)
 
     piece = queries // cols
     copies = []
@@ -301,6 +352,80 @@
         )
         cp.start()
         copies.append(cp)
+
+    if fused:
+
+        def hop_b(k, carry):
+            t = spot(ahead(k), a, 1 - b)
+            copy_a1(k, t).wait_recv()
+            dp[t] += rs1[k]
+            copy_b1(k, t).start()
+            return carry
+
+        lax.fori_loop(0, depth, hop_b, 0)
+
+        def hop_z(k, carry):
+            t = spot(ahead(k), a, b)
+            copy_a1(depth + k, t).wait_recv()
+            copy_b1(k, t).wait_recv()
+            dp[t] += rs1[depth + k] + rs2[k]
+            if depth > 1:
+
+                @pl.when(k < depth - 1)
+                def _():
+                    copy_z1(k, t).start()
+
+            return carry
+
+        lax.fori_loop(0, depth, hop_z, 0)
+        total = dp[r]
+        for k in range(depth - 1):
+            copy_z1(k, r).wait_recv()
+            total = total + rs3[k]
+        unit = phat[r].astype(jnp.float32).T
+        along = jnp.sum(unit * total, axis=0, keepdims=True)
+        dp_out[r] = ((total - unit * along) / plen[r]).T
+
+        def copy_a2(i, t):
+            return push(dp_out.at[t], dp_out.at[t], as_.at[i], ar.at[i], (peer_a, c))
+
+        def copy_b2(m, t):
+            return push(dp_out.at[t], dp_out.at[t], bs.at[m], br.at[m], (peer_b, c))
+
+        def copy_z2(k, t):
+            return push(
+                dp_out.at[t], dp_out.at[t], zs.at[k], zr.at[k], (spot(ahead(k), a, b), c)
+            )
+
+        def behind(m):
+            return lax.rem(z + depth - m, depth)
+
+        copy_a2(0, r).start()
+        copy_b2(0, r).start()
+        for k in range(depth - 1):
+            copy_z2(k, r).start()
+        for m in range(depth):
+            if m > 0:
+                t = spot(behind(m), a, b)
+                copy_z2(m - 1, t).wait_recv()
+                copy_b2(m, t).start()
+                copy_a2(2 * m, t).start()
+            t = spot(behind(m), a, 1 - b)
+            copy_b2(m, t).wait_recv()
+            copy_a2(2 * m + 1, t).start()
+        for m in range(depth):
+            copy_a2(2 * m, spot(behind(m), 1 - a, b)).wait_recv()
+            copy_a2(2 * m + 1, spot(behind(m), 1 - a, 1 - b)).wait_recv()
+        for k in range(2 * depth):
+            copy_a1(k, r).wait_send()
+            copy_a2(k, r).wait_send()
+        for k in range(depth):
+            copy_b1(k, r).wait_send()
+            copy_b2(k, r).wait_send()
+        for k in range(depth - 1):
+            copy_z1(k, r).wait_send()
+            copy_z2(k, r).wait_send()
+
     for cp in copies:
         cp.wait()
     mine = dqacc[pl.ds(pl.multiple_of(c * piece, 8), piece), :]
@@ -309,20 +434,29 @@
     dq_out[...] = mine
 
 
-def run_main(rows, cols, qhat, scaled, phat, offset, wgt, left_t):
+def run_main(rows, cols, fused, qhat, scaled, phat, offset, wgt, left_t, plen):
     queries, feats = qhat.shape
     tiles, width, _ = phat.shape
     f32 = jnp.float32
     vec = lambda *s: pltpu.VMEM(s, f32)
     sems_r = [pltpu.SemaphoreType.DMA((rows,))] * 2
     sems_c = [pltpu.SemaphoreType.DMA((cols,))] * 2
+    ring = []
+    if fused:
+        depth = rows // 4
+        ring = [
+            vec(tiles, feats, width), vec(2 * depth, feats, width),
+            vec(depth, feats, width), vec(depth, feats, width),
+        ]
+        for count in (2, 1, 1, 2, 1, 1):
+            ring += [pltpu.SemaphoreType.DMA((count * depth,))] * 2
     return pl.pallas_call(
-        functools.partial(main_kernel, rows, cols),
+        functools.partial(main_kernel, rows, cols, fused),
         out_shape=(
-            jax.ShapeDtypeStruct((tiles, feats, width), f32),
+            jax.ShapeDtypeStruct((tiles, width, feats) if fused else (tiles, feats, width), f32),
             jax.ShapeDtypeStruct((queries // cols, feats), f32),
         ),
-        in_specs=[pl.BlockSpec(memory_space=pltpu.VMEM)] * 6,
+        in_specs=[pl.BlockSpec(memory_space=pltpu.VMEM)] * 7,
         out_specs=(pl.BlockSpec(memory_space=pltpu.VMEM),) * 2,
         scratch_shapes=[
             vec(tiles, queries, width), vec(tiles, queries, width),
@@ -332,12 +466,12 @@
             vec(tiles, 1, width), vec(rows, 1, width), vec(tiles, 1, width),
             vec(1, width), vec(queries, feats), vec(cols, queries, LANES),
         ]
-        + sems_c + sems_r + sems_r + sems_c + sems_r + sems_r + sems_c,
+        + sems_c + sems_r + sems_r + sems_c + sems_r + sems_r + sems_c + ring,
         compiler_params=pltpu.CompilerParams(
             collective_id=0, has_side_effects=True, vmem_limit_bytes=56 * 1024 * 1024
         ),
         name="transport_sweeps",
-    )(qhat, scaled, phat, offset, wgt, left_t)
+    )(qhat, scaled, phat, offset, wgt, left_t, plen)
 
 
 def local(rows, cols, queries, prototypes, potential, weights, capacity, cotangent):
@@ -348,11 +482,13 @@
     slots, feats = phat.shape
     width, tiles = tiles_of(slots, rows)
     offset = jnp.log2(capacity.astype(jnp.float32)) - potential * (1.0 / (TEMPER * math.log(2.0)))
+    fused = tiles == rows and rows % 4 == 0
     dp, dq = run_main(
-        rows, cols, qhat, scaled, phat.reshape(tiles, width, feats),
+        rows, cols, fused, qhat, scaled, phat.reshape(tiles, width, feats),
         offset.reshape(tiles, 1, width),
         jnp.broadcast_to(wgt[:, None], (wgt.shape[0], LANES))[:, :1],
         jnp.stack([qhat.T, scaled.T]),
+        plen.reshape(tiles, 1, width),
     )
     piece = dq.shape[0]
     begin = lax.axis_index("cols") * piece
@@ -361,6 +497,8 @@
         lax.dynamic_slice_in_dim(qhat, begin, piece, 0),
         lax.dynamic_slice_in_dim(qlen, begin, piece, 0),
     )
+    if fused:
+        return (grad_queries, dp.reshape(slots, feats))
     whole = lax.psum(dp, "rows")
     whole = whole.transpose(0, 2, 1).reshape(slots, feats)
     grad_protos = unit_back(whole, phat, plen)

time: 265 us -> 158 us (0.60)
  the two profiles are of different devices: /device:TPU:0 before, /device:TPU:16 now
where the time goes in v2:
time: 158 us
  Pallas kernels  139 us (88%)
  local copies, waits for them, and re-layouts  10.8 us (7%)
  other arithmetic  7.79 us (5%)
    pallas_call x1, Pallas kernels, run_main(): pl.pallas_call(functools.partial(main_kernel, rows, cols, fused), out_sha...  139 us
    unnamed x12, local copies, waits for them, and re-layouts  7.41 us
    convert_element_type x2, other arithmetic, unit_rows(): return ((wide / length[:, None]).astype(jnp.bfloat16), length)  4.39 us

profile of v2, /device:TPU:16, one launch (start us, length us, event | category | flops | bytes accessed | tf_op | source)
XLA Modules:
  0.0 158.2 jit_solution(15183272892003057924)
XLA Ops:
  0.6 0.0 copy-start
  0.6 1.2 copy.15
  1.9 0.7 convert_element_type.30
  2.6 1.0 copy.16
  3.6 0.0 copy-start.2
  3.6 0.0 copy-start.3
  3.7 0.7 pad_maximum_fusion.left_t
  4.4 0.8 copy.17.qhat
  5.2 0.8 copy.18.scaled
  6.0 0.8 copy.19.wgt
  6.8 0.0 copy-done
  6.8 1.2 fusion
  8.0 0.0 copy-start.1
  8.0 4.4 %fusion.1 = bf16[8192,128]{1,0:T(8,128)(2,1)} fusion(bf16[8192,128]{1,0:T(8,128)(2,1)S(1)} %copy-done, f32[8192]{0:T(1024)S(1)} %add_sqrt_fusion), kind=kLoop, calls=%fused_computation.3 | loop fusion | flops 3145728 | bytes 4227072 | tf_op jit(solution)/shard_map/convert_element_type | solution.py:19
  12.4 0.0 copy-done.2
  12.4 0.0 copy-done.3
  12.4 0.6 multiply_subtract_fusion
  13.0 0.0 copy-done.1
  13.0 138.8 %transport_sweeps.1 = (f32[16,512,128]{2,1,0:T(8,128)}, f32[256,128]{1,0:T(8,128)}) custom-call(bf16[512,128]{1,0:T(8,128)(2,1)} %copy.17.qhat, bf16[512,128]{1,0:T(8,128)(2,1)} %copy.18.scaled, bf16[16,512,128]{2,1,0:T(8,128)(2,1)} %bitcast.13, f32[16,1,512]{2,1,0:T(1,128)} %bitcast.16, f32[512,1]{1,0:T(8,128)} %copy.19.wgt, ...), custom_call_target="tpu_custom_call" | custom-call | tf_op jit(solution)/shard_map/transport_sweeps/pallas_call | solution.py:453
  151.8 1.0 copy.21
  152.9 0.1 dynamic_slice.7
  153.0 0.8 copy.22
  153.8 4.5 %copy.24 = f32[8192,128]{1,0:T(8,128)} copy(f32[8192,128]{1,0:T(8,128)} %bitcast.14) | data formatting | bytes 8388608
  (9 shorter events, 0.3 us)
Async XLA Ops:
  0.6 6.2 %copy-start = (bf16[8192,128]{1,0:T(8,128)(2,1)S(1)}, bf16[8192,128]{1,0:T(8,128)(2,1)}, u32[]{:S(2)}) copy-start(bf16[8192,128]{1,0:T(8,128)(2,1)} %param.7) | copy-start | bytes 6291460
  3.6 8.7 %copy-start.2 = (f32[8192]{0:T(1024)S(1)}, f32[8192]{0:T(1024)}, u32[]{:S(2)}) copy-start(f32[8192]{0:T(1024)} %param.8) | copy-start | bytes 98308
  3.6 8.7 %copy-start.3 = (s32[8192]{0:T(1024)S(1)}, s32[8192]{0:T(1024)}, u32[]{:S(2)}) copy-start(s32[8192]{0:T(1024)} %param.10) | copy-start | bytes 98308
  8.0 5.0 %copy-start.1 = (f32[8192]{0:T(1024)}, f32[8192]{0:T(1024)S(1)}, u32[]{:S(2)}) copy-start(f32[8192]{0:T(1024)S(1)} %add_sqrt_fusion) | copy-start | bytes 98308

commit v3 on v1

--- a/solution.py
+++ b/solution.py
@@ -15,14 +15,14 @@
 
 def unit_rows(matrix):
     wide = matrix.astype(jnp.float32)
-    length = jnp.sqrt(jnp.sum(wide * wide, axis=1) + 1e-06)
-    return ((wide / length[:, None]).astype(jnp.bfloat16), length)
+    length = jnp.sqrt(jnp.sum(wide * wide, axis=1, keepdims=True) + 1e-06)
+    return ((wide / length).astype(jnp.bfloat16), length)
 
 
 def unit_back(grad, unit, length):
     wide = unit.astype(jnp.float32)
     along = jnp.sum(wide * grad, axis=1, keepdims=True)
-    return (grad - wide * along) / length[:, None]
+    return (grad - wide * along) / length
 
 
 def nt_dot(left, right):
@@ -44,11 +44,12 @@
 
 
 def main_kernel(
-    rows, cols, qhat, scaled, phat, offset, wgt, left_t, dp_out, dq_out,
+    rows, cols, fused, queries_in, protos_in, potential, weights, capacity, cotangent,
+    dp_out, dq_out, qhat, scaled, phat, offset, wgt, left_t,
     kern, coup, zacc, kacc, share, alpha, cbuf, part, pbuf, beta, gpart, gbuf, shift,
     invs, dqacc, dqbuf,
     csend, crecv, psend, precv, bsend, brecv, rsend, rrecv, gsend, grecv, hsend, hrecv,
-    dsend, drecv,
+    dsend, drecv, *ring,
 ):
     tiles, queries, width = kern.shape
     lanes = [slice(k, k + LANES) for k in range(0, width, LANES)]
@@ -70,9 +71,19 @@
     dqacc[...] = jnp.zeros_like(dqacc)
     log2e = 1.0 / (TEMPER * math.log(2.0))
     step = min(queries, 256)
+    offset[...] = jnp.log2(capacity[...].astype(jnp.float32)) - potential[...] * log2e
+    feats = qhat.shape[1]
+    wgt[...] = jnp.broadcast_to(weights[...].astype(jnp.float32), (feats, queries)).T
+    unit, _ = unit_rows(queries_in[...])
+    qhat[...] = unit
+    left_t[0] = unit.astype(jnp.float32).T.astype(jnp.bfloat16)
+    unit = (cotangent[...].astype(jnp.float32) / wgt[...]).astype(jnp.bfloat16)
+    scaled[...] = unit
+    left_t[1] = unit.astype(jnp.float32).T.astype(jnp.bfloat16)
 
     def first(t, carry):
-        proto = phat[t]
+        proto, _ = unit_rows(protos_in[t])
+        phat[t] = proto
         base = offset[t]
         for q in range(0, queries, step):
             qs = slice(q, q + step)
@@ -117,7 +128,7 @@
     total = over_cols(csend, crecv)
     ztot = total[:, 0:1]
     kgsum = total[:, 1:2]
-    w = wgt[...]
+    w = wgt[:, 0:1]
     srate = w / ztot
     share[...] = jnp.broadcast_to(srate, share.shape)
     alpha[...] = jnp.broadcast_to(srate * kgsum / w, alpha.shape)
@@ -270,7 +281,12 @@
     own(second_beta)
     spread(shift, hsend, hrecv)
 
-    def fifth(t, carry):
+    if fused:
+        dp, rs1, rs2, rs3, s1s, s1r, s2s, s2r, s3s, s3r, as_, ar, bs, br, zs, zr = ring
+    else:
+        dp = dp_out
+
+    def fifth(t):
         ds = []
         pb = []
         for l in lanes:
@@ -284,12 +300,76 @@
         ds = jnp.concatenate(ds, axis=1)
         pb = jnp.concatenate(pb, axis=1)
         dqacc[...] += jnp.dot(ds, phat[t], preferred_element_type=jnp.float32)
-        dp_out[t] = jnp.dot(
+        grad = jnp.dot(
             left_t[0], ds, preferred_element_type=jnp.float32
         ) + jnp.dot(left_t[1], pb, preferred_element_type=jnp.float32)
-        return carry
-
-    lax.fori_loop(0, tiles, fifth, 0)
+        if fused:
+            for h, l in enumerate(lanes):
+                dp[t, h] = grad[:, l]
+        else:
+            dp[t] = grad
+
+    if not fused:
+
+        def plain(t, carry):
+            fifth(t)
+            return carry
+
+        lax.fori_loop(0, tiles, plain, 0)
+    else:
+        depth = rows // 4
+        z = r // 4
+        even = lax.rem(c, 2) == 0
+        wa = jnp.where(even, 1, 2)
+        wb = 3 - wa
+        a = jnp.where(even, lax.rem(r, 2), lax.rem(r // 2, 2))
+        b = jnp.where(even, lax.rem(r // 2, 2), lax.rem(r, 2))
+        peer_a = r + (1 - 2 * a) * wa
+        peer_b = r + (1 - 2 * b) * wb
+
+        def spot(zz, av, bv):
+            return zz * 4 + av * wa + bv * wb
+
+        def ahead(k):
+            return lax.rem(z + 1 + k, depth)
+
+        def copy_a1(i, t, h):
+            return push(dp.at[t, h], rs1.at[i, h], s1s.at[i, h], s1r.at[i, h], (peer_a, c))
+
+        def copy_b1(k, t, h):
+            return push(dp.at[t, h], rs2.at[k, h], s2s.at[k, h], s2r.at[k, h], (peer_b, c))
+
+        def copy_z1(k, t, h):
+            return push(
+                dp.at[t, h], rs3.at[k, h], s3s.at[k, h], s3r.at[k, h],
+                (spot(ahead(k), a, b), c),
+            )
+
+        def away(i):
+            return spot(ahead(lax.rem(i, depth)), 1 - a, jnp.where(i < depth, 1 - b, b))
+
+        def leave(i, carry):
+            t = away(i)
+            fifth(t)
+            copy_a1(i, t, 0).start()
+            return carry
+
+        lax.fori_loop(0, 2 * depth, leave, 0)
+
+        def leave_piece(h):
+            def each(i, carry):
+                copy_a1(i, away(i), h).start()
+                return carry
+
+            lax.fori_loop(0, 2 * depth, each, 0)
+
+        leave_piece(1)
+
+        def stay(i, carry):
+            fifth(spot(ahead(lax.rem(i, depth)), a, jnp.where(i < depth, 1 - b, b)))
+            return carry
+
+        lax.fori_loop(0, 2 * depth, stay, 0)
 
     piece = queries // cols
     copies = []
@@ -301,30 +381,143 @@
         )
         cp.start()
         copies.append(cp)
+
+    if fused:
+        count = len(lanes)
+
+        def hop_b(h):
+            def each(k, carry):
+                t = spot(ahead(k), a, 1 - b)
+                copy_a1(k, t, h).wait_recv()
+                dp[t, h] += rs1[k, h]
+                copy_b1(k, t, h).start()
+                return carry
+
+            lax.fori_loop(0, depth, each, 0)
+
+        def hop_z(h):
+            def each(k, carry):
+                t = spot(ahead(k), a, b)
+                copy_a1(depth + k, t, h).wait_recv()
+                copy_b1(k, t, h).wait_recv()
+                dp[t, h] += rs1[depth + k, h] + rs2[k, h]
+
+                @pl.when(k < depth - 1)
+                def _():
+                    copy_z1(k, t, h).start()
+
+                return carry
+
+            lax.fori_loop(0, depth, each, 0)
+
+        def block(t, h):
+            return dp_out.at[t, pl.ds(h * LANES, LANES)]
+
+        def copy_a2(i, t, h):
+            return push(block(t, h), block(t, h), as_.at[i, h], ar.at[i, h], (peer_a, c))
+
+        def copy_b2(m, t, h):
+            return push(block(t, h), block(t, h), bs.at[m, h], br.at[m, h], (peer_b, c))
+
+        def copy_z2(k, t, h):
+            return push(
+                block(t, h), block(t, h), zs.at[k, h], zr.at[k, h],
+                (spot(ahead(k), a, b), c),
+            )
+
+        def behind(m):
+            return lax.rem(z + depth - m, depth)
+
+        def settle(h):
+            total = dp[r, h]
+            for k in range(depth - 1):
+                copy_z1(k, r, h).wait_recv()
+                total = total + rs3[k, h]
+            rows_h = pl.ds(h * LANES, LANES)
+            unit, length = unit_rows(protos_in[r, rows_h])
+            dp_out[r, rows_h] = unit_back(total.T, unit, length)
+            copy_a2(0, r, h).start()
+            copy_b2(0, r, h).start()
+            for k in range(depth - 1):
+                copy_z2(k, r, h).start()
+
+        def pass_z(h):
+            t = spot(z, a, 1 - b)
+            copy_b2(0, t, h).wait_recv()
+            copy_a2(1, t, h).start()
+            for m in range(1, depth):
+                t = spot(behind(m), a, b)
+                copy_z2(m - 1, t, h).wait_recv()
+                copy_b2(m, t, h).start()
+                copy_a2(2 * m, t, h).start()
+
+        def pass_b(h):
+            for m in range(1, depth):
+                t = spot(behind(m), a, 1 - b)
+                copy_b2(m, t, h).wait_recv()
+                copy_a2(2 * m + 1, t, h).start()
+
+        for s in range(count + 4):
+            if 2 <= s + 2 < count:
+                leave_piece(s + 2)
+            for lag, stage in ((4, pass_b), (3, pass_z), (2, settle), (1, hop_z), (0, hop_b)):
+                if 0 <= s - lag < count:
+                    stage(s - lag)
+
+        def finish(h):
+            for m in range(depth):
+                copy_a2(2 * m, spot(behind(m), 1 - a, b), h).wait_recv()
+                copy_a2(2 * m + 1, spot(behind(m), 1 - a, 1 - b), h).wait_recv()
+            for k in range(2 * depth):
+                copy_a1(k, r, h).wait_send()
+                copy_a2(k, r, h).wait_send()
+            for k in range(depth):
+                copy_b1(k, r, h).wait_send()
+                copy_b2(k, r, h).wait_send()
+            for k in range(depth - 1):
+                copy_z1(k, r, h).wait_send()
+                copy_z2(k, r, h).wait_send()
+
+        for h in range(count):
+            finish(h)
+
     for cp in copies:
         cp.wait()
-    mine = dqacc[pl.ds(pl.multiple_of(c * piece, 8), piece), :]
+    begin = pl.ds(pl.multiple_of(c * piece, 16), piece)
+    mine = dqacc[begin, :]
     for o in range(1, cols):
         mine = mine + cbuf[o, 0:piece]
-    dq_out[...] = mine
-
-
-def run_main(rows, cols, qhat, scaled, phat, offset, wgt, left_t):
-    queries, feats = qhat.shape
-    tiles, width, _ = phat.shape
+    unit, length = unit_rows(queries_in[begin, :])
+    dq_out[...] = unit_back(mine, unit, length)
+
+
+def run_main(rows, cols, fused, *args):
+    queries, feats = args[0].shape
+    tiles, width, _ = args[1].shape
+    bf16 = jnp.bfloat16
     f32 = jnp.float32
     vec = lambda *s: pltpu.VMEM(s, f32)
     sems_r = [pltpu.SemaphoreType.DMA((rows,))] * 2
     sems_c = [pltpu.SemaphoreType.DMA((cols,))] * 2
+    ring = []
+    if fused:
+        depth = rows // 4
+        cuts = width // LANES
+        ring = [vec(n, cuts, feats, LANES) for n in (tiles, 2 * depth, depth, depth)]
+        for count in (2, 1, 1, 2, 1, 1):
+            ring += [pltpu.SemaphoreType.DMA((count * depth, cuts))] * 2
     return pl.pallas_call(
-        functools.partial(main_kernel, rows, cols),
+        functools.partial(main_kernel, rows, cols, fused),
         out_shape=(
-            jax.ShapeDtypeStruct((tiles, feats, width), f32),
+            jax.ShapeDtypeStruct((tiles, width, feats) if fused else (tiles, feats, width), f32),
             jax.ShapeDtypeStruct((queries // cols, feats), f32),
         ),
         in_specs=[pl.BlockSpec(memory_space=pltpu.VMEM)] * 6,
         out_specs=(pl.BlockSpec(memory_space=pltpu.VMEM),) * 2,
         scratch_shapes=[
+            pltpu.VMEM((queries, feats), bf16), pltpu.VMEM((queries, feats), bf16),
+            pltpu.VMEM((tiles, width, feats), bf16), vec(tiles, 1, width),
+            vec(queries, LANES), pltpu.VMEM((2, feats, queries), bf16),
             vec(tiles, queries, width), vec(tiles, queries, width),
             vec(queries, LANES), vec(queries, LANES), vec(queries, LANES), vec(queries, LANES),
             vec(cols, queries, LANES),
@@ -332,39 +525,28 @@
             vec(tiles, 1, width), vec(rows, 1, width), vec(tiles, 1, width),
             vec(1, width), vec(queries, feats), vec(cols, queries, LANES),
         ]
-        + sems_c + sems_r + sems_r + sems_c + sems_r + sems_r + sems_c,
+        + sems_c + sems_r + sems_r + sems_c + sems_r + sems_r + sems_c + ring,
         compiler_params=pltpu.CompilerParams(
             collective_id=0, has_side_effects=True, vmem_limit_bytes=56 * 1024 * 1024
         ),
         name="transport_sweeps",
-    )(qhat, scaled, phat, offset, wgt, left_t)
+    )(*args)
 
 
 def local(rows, cols, queries, prototypes, potential, weights, capacity, cotangent):
-    qhat, qlen = unit_rows(queries)
-    phat, plen = unit_rows(prototypes)
-    wgt = weights.astype(jnp.float32)
-    scaled = (cotangent.astype(jnp.float32) / wgt[:, None]).astype(jnp.bfloat16)
-    slots, feats = phat.shape
+    slots, feats = prototypes.shape
     width, tiles = tiles_of(slots, rows)
-    offset = jnp.log2(capacity.astype(jnp.float32)) - potential * (1.0 / (TEMPER * math.log(2.0)))
+    fused = tiles == rows and rows % 4 == 0
     dp, dq = run_main(
-        rows, cols, qhat, scaled, phat.reshape(tiles, width, feats),
-        offset.reshape(tiles, 1, width),
-        jnp.broadcast_to(wgt[:, None], (wgt.shape[0], LANES))[:, :1],
-        jnp.stack([qhat.T, scaled.T]),
+        rows, cols, fused, queries, prototypes.reshape(tiles, width, feats),
+        potential.reshape(tiles, 1, width), weights.reshape(1, -1),
+        capacity.reshape(tiles, 1, width), cotangent,
     )
-    piece = dq.shape[0]
-    begin = lax.axis_index("cols") * piece
-    grad_queries = unit_back(
-        dq,
-        lax.dynamic_slice_in_dim(qhat, begin, piece, 0),
-        lax.dynamic_slice_in_dim(qlen, begin, piece, 0),
-    )
+    if fused:
+        return (dq, dp.reshape(slots, feats))
     whole = lax.psum(dp, "rows")
     whole = whole.transpose(0, 2, 1).reshape(slots, feats)
-    grad_protos = unit_back(whole, phat, plen)
-    return (grad_queries, grad_protos)
+    return (dq, unit_back(whole, *unit_rows(prototypes)))
 
 
 def solution(mesh):

time: 265 us -> 127 us (0.48)
  waiting for transfers between devices: 167 us -> 0 us
  Pallas kernels: 53.3 us -> 120 us
  other arithmetic: 19.2 us -> 0 us
  between operations: 14.2 us -> 0.64 us
  local copies, waits for them, and re-layouts: 11.7 us -> 6.04 us
    psum x1 -> x0, waiting for transfers between devices: 167 us -> none  [local(): whole = lax.psum(dp, 'rows')]
    pallas_call x1, Pallas kernels: 53.3 us -> 120 us  [run_main(): pl.pallas_call(functools.partial(main_kernel, rows, cols, fused), out_sha...]
    reduce_sum x4 -> x0, other arithmetic: 7.02 us -> none  [the longest x2 4.23 us: unit_back(): along = jnp.sum(wide * grad, axis=1, keepdims=True)]
    div x2 -> x0, other arithmetic: 5.62 us -> none  [unit_back(): return (grad - wide * along) / length[:, None]]
    transpose x1 -> x0, local copies, waits for them, and re-layouts: 5.32 us -> none  [local(): whole = whole.transpose(0, 2, 1).reshape(slots, feats)]
    convert_element_type x4 -> x0, other arithmetic: 5.1 us -> none  [the longest x2 4.39 us: unit_rows(): return ((wide / length[:, None]).astype(jnp.bfloat16), length)]
    unnamed x13 -> x2, local copies, waits for them, and re-layouts: 3.81 us -> 6.04 us
  transfers between devices with their start and end apart: 1 -> 0, of which waited for: 1 -> 0; matrix products, arithmetic and copies ran while one was open for 0% -> 0% of each run, Pallas kernels for 0% -> 0%
where the time goes in v3:
time: 127 us
  Pallas kernels  120 us (94%)
  local copies, waits for them, and re-layouts  6.04 us (5%)
    pallas_call x1, Pallas kernels, run_main(): pl.pallas_call(functools.partial(main_kernel, rows, cols, fused), out_sha...  120 us
    unnamed x2, local copies, waits for them, and re-layouts  6.04 us

profile of v3, /device:TPU:0, one launch (start us, length us, event | category | flops | bytes accessed | tf_op | source)
XLA Modules:
  0.0 127.1 jit_solution(14534217593002435260)
XLA Ops:
  0.6 120.5 %transport_sweeps.1 = (f32[16,512,128]{2,1,0:T(8,128)}, f32[256,128]{1,0:T(8,128)}) custom-call(bf16[512,128]{1,0:T(8,128)(2,1)} %queries_in.1, bf16[16,512,128]{2,1,0:T(8,128)(2,1)} %bitcast.6, f32[16,1,512]{2,1,0:T(1,128)} %bitcast.7, s32[1,512]{1,0:T(1,128)} %bitcast.9, s32[16,1,512]{2,1,0:T(1,128)} %bitcast.8, bf16[512,128]{1,0:T(8,128)(2,1)} %cotangent.1), custom_call_target="tpu_custom_call" | custom-call | tf_op jit(solution)/shard_map/transport_sweeps/pallas_call | solution.py:509
  121.1 1.6 %copy.10 = f32[256,128]{1,0:T(8,128)} copy(f32[256,128]{1,0:T(8,128)} %get-tuple-element.8) | data formatting | bytes 262144
  122.7 4.5 %copy.11 = f32[8192,128]{1,0:T(8,128)} copy(f32[8192,128]{1,0:T(8,128)} %bitcast.5) | data formatting | bytes 8388608

commit v4 on v3

--- a/solution.py
+++ b/solution.py
@@ -47,7 +47,7 @@
     rows, cols, fused, queries_in, protos_in, potential, weights, capacity, cotangent,
     dp_out, dq_out, qhat, scaled, phat, offset, wgt, left_t,
     kern, coup, zacc, kacc, share, alpha, cbuf, part, pbuf, beta, gpart, gbuf, shift,
-    invs, dqacc, dqbuf,
+    invs, dqacc, dqbuf, rbuf,
     csend, crecv, psend, precv, bsend, brecv, rsend, rrecv, gsend, grecv, hsend, hrecv,
     dsend, drecv, *ring,
 ):
@@ -104,36 +104,61 @@
     lax.fori_loop(0, tiles, first, 0)
     pl.semaphore_wait(barrier, rows - 1 + cols - 1)
 
-    lane = lax.broadcasted_iota(jnp.int32, (queries, LANES), 1)
-
-    def over_cols(send, recv):
+    def tall(row):
+        return jnp.broadcast_to(row, (LANES, queries)).T
+
+    def flat(acc):
+        return jnp.sum(acc[...].T, axis=0, keepdims=True)
+
+    def over_cols(buf, send, recv):
         copies = []
         for o in range(1, cols):
             cp = push(
-                cbuf.at[0], cbuf.at[o], send.at[o], recv.at[o],
-                (r, lax.rem(c + o, cols)),
+                buf.at[0], buf.at[o], send.at[o], recv.at[o], (r, lax.rem(c + o, cols))
             )
             cp.start()
             copies.append(cp)
         for cp in copies:
             cp.wait()
-        total = cbuf[0]
+        total = buf[0]
         for o in range(1, cols):
-            total = total + cbuf[o]
+            total = total + buf[o]
         return total
 
-    ztot = jnp.sum(zacc[...], axis=1, keepdims=True)
-    kgsum = jnp.sum(kacc[...], axis=1, keepdims=True)
-    cbuf[0] = jnp.where(lane == 0, ztot, kgsum)
-    total = over_cols(csend, crecv)
-    ztot = total[:, 0:1]
-    kgsum = total[:, 1:2]
-    w = wgt[:, 0:1]
-    srate = w / ztot
-    share[...] = jnp.broadcast_to(srate, share.shape)
-    alpha[...] = jnp.broadcast_to(srate * kgsum / w, alpha.shape)
-
-    def second(t, carry):
+    cbuf[0, 0:1] = flat(zacc)
+    cbuf[0, 1:2] = flat(kacc)
+    total = over_cols(cbuf, csend, crecv)
+    w = weights[...].astype(jnp.float32)
+    srate = w / total[0:1]
+    share[...] = tall(srate)
+    alpha[...] = tall(srate * total[1:2] / w)
+    direct = tiles == rows
+
+    def swept(body, part_ref, buf, send, recv):
+        if not direct:
+            lax.fori_loop(0, tiles, lambda t, k: body(t) or k, 0)
+            scatter(part_ref, buf, send, recv)
+            return
+
+        def each(o, carry):
+            t = lax.rem(r + o, rows)
+            body(t)
+
+            @pl.when(o < rows)
+            def _():
+                push(part_ref.at[t], buf.at[o], send.at[o], recv.at[o], (t, c)).start()
+
+            return carry
+
+        lax.fori_loop(1, rows + 1, each, 0)
+
+        def done(o, carry):
+            push(part_ref.at[r], buf.at[o], send.at[o], recv.at[o], (lax.rem(r + o, rows), c)).wait()
+            return carry
+
+        lax.fori_loop(1, rows, done, 0)
+
+    def second(t):
         for l in lanes:
             p = share[...] * kern[t, :, l]
             kern[t, :, l] = p
@@ -141,9 +166,6 @@
             part[t, 1:2, l] = jnp.sum(
                 p * (coup[t, :, l] - alpha[...]), axis=0, keepdims=True
             )
-        return carry
-
-    lax.fori_loop(0, tiles, second, 0)
 
     def scatter(src, dst, send, recv):
         def each(o, carry):
@@ -179,7 +201,7 @@
 
         lax.fori_loop(1, rows, done, 0)
 
-    def spread(buf, send, recv):
+    def spread_start(buf, send, recv):
         def each(o, carry):
             peer = lax.rem(r + o, rows)
 
@@ -194,6 +216,23 @@
 
         lax.fori_loop(1, rows, each, 0)
 
+    def spread_got(buf, send, recv, t):
+        o = lax.rem(r + rows - t, rows)
+
+        @pl.when(o > 0)
+        def _():
+            push(buf.at[t], buf.at[t], send.at[o], recv.at[o], (t, c)).wait_recv()
+
+    def spread_sent(buf, send, recv):
+        def done(o, carry):
+            push(
+                buf.at[r], buf.at[r], send.at[o], recv.at[o], (lax.rem(r + o, rows), c)
+            ).wait_send()
+            return carry
+
+        lax.fori_loop(1, rows, done, 0)
+
+    def spread_wait(buf, send, recv):
         def done(o, carry):
             origin = lax.rem(r + rows - o, rows)
             peer = lax.rem(r + o, rows)
@@ -222,7 +261,7 @@
         else:
             pl.when(r < tiles)(body)
 
-    scatter(part, pbuf, psend, precv)
+    swept(second, part, pbuf, psend, precv)
 
     def first_beta():
         both = part[r]
@@ -233,11 +272,16 @@
         beta[r] = both[1:2] * inv
 
     own(first_beta)
-    spread(beta, bsend, brecv)
-
     zacc[...] = jnp.zeros_like(zacc)
-
-    def third(t, carry):
+    spread_start(beta, bsend, brecv)
+    if not direct:
+        spread_wait(beta, bsend, brecv)
+
+    def third(o, carry):
+        t = o
+        if direct:
+            t = lax.rem(r + rows - o, rows)
+            spread_got(beta, bsend, brecv, t)
         acc = zacc[...]
         for l in lanes:
             acc = acc + kern[t, :, l] * beta[t, :, l]
@@ -245,32 +289,16 @@
         return carry
 
     lax.fori_loop(0, tiles, third, 0)
-    rowprod = jnp.sum(zacc[...], axis=1, keepdims=True)
-    cbuf2 = jnp.broadcast_to(rowprod, (queries, LANES))
-    kacc[...] = cbuf2
-    copies = []
-    for o in range(1, cols):
-        cp = push(
-            kacc, dqbuf.at[o], rsend.at[o], rrecv.at[o], (r, lax.rem(c + o, cols))
-        )
-        cp.start()
-        copies.append(cp)
-    for cp in copies:
-        cp.wait()
-    rowtot = kacc[...]
-    for o in range(1, cols):
-        rowtot = rowtot + dqbuf[o]
-    change = rowtot / w
+    rbuf[0] = flat(zacc)
+    change = tall(over_cols(rbuf, rsend, rrecv) / w)
     share[...] = change
     alpha[...] = alpha[...] - change
 
-    def fourth(t, carry):
+    def fourth(t):
         for l in lanes:
             gpart[t, :, l] = jnp.sum(share[...] * kern[t, :, l], axis=0, keepdims=True)
-        return carry
-
-    lax.fori_loop(0, tiles, fourth, 0)
-    scatter(gpart, gbuf, gsend, grecv)
+
+    swept(fourth, gpart, gbuf, gsend, grecv)
 
     def second_beta():
         tot = gpart[r]
@@ -279,7 +307,9 @@
         shift[r] = beta[r] + tot * invs[...]
 
     own(second_beta)
-    spread(shift, hsend, hrecv)
+    spread_start(shift, hsend, hrecv)
+    if not direct:
+        spread_wait(shift, hsend, hrecv)
 
     if fused:
         dp, rs1, rs2, rs3, s1s, s1r, s2s, s2r, s3s, s3r, as_, ar, bs, br, zs, zr = ring
@@ -287,6 +317,8 @@
         dp = dp_out
 
     def fifth(t):
+        if direct:
+            spread_got(shift, hsend, hrecv, t)
         ds = []
         pb = []
         for l in lanes:
@@ -377,7 +409,7 @@
         peer = lax.rem(c + o, cols)
         cp = push(
             dqacc.at[pl.ds(pl.multiple_of(peer * piece, 8), piece)],
-            cbuf.at[o, pl.ds(0, piece)], dsend.at[o], drecv.at[o], (r, peer),
+            dqbuf.at[o], dsend.at[o], drecv.at[o], (r, peer),
         )
         cp.start()
         copies.append(cp)
@@ -481,12 +513,15 @@
         for h in range(count):
             finish(h)
 
+    if direct:
+        spread_sent(beta, bsend, brecv)
+        spread_sent(shift, hsend, hrecv)
     for cp in copies:
         cp.wait()
     begin = pl.ds(pl.multiple_of(c * piece, 16), piece)
     mine = dqacc[begin, :]
     for o in range(1, cols):
-        mine = mine + cbuf[o, 0:piece]
+        mine = mine + dqbuf[o]
     unit, length = unit_rows(queries_in[begin, :])
     dq_out[...] = unit_back(mine, unit, length)
 
@@ -520,10 +555,11 @@
             vec(queries, LANES), pltpu.VMEM((2, feats, queries), bf16),
             vec(tiles, queries, width), vec(tiles, queries, width),
             vec(queries, LANES), vec(queries, LANES), vec(queries, LANES), vec(queries, LANES),
-            vec(cols, queries, LANES),
+            vec(cols, 2, queries),
             vec(tiles, 2, width), vec(rows, 2, width), vec(tiles, 1, width),
             vec(tiles, 1, width), vec(rows, 1, width), vec(tiles, 1, width),
-            vec(1, width), vec(queries, feats), vec(cols, queries, LANES),
+            vec(1, width), vec(queries, feats),
+            vec(cols, queries // cols, feats), vec(cols, 1, queries),
         ]
         + sems_c + sems_r + sems_r + sems_c + sems_r + sems_r + sems_c + ring,
         compiler_params=pltpu.CompilerParams(
@@ -531,6 +567,32 @@
         ),
         name="transport_sweeps",
     )(*args)
+
+
+def hand_over(dp, dq, dp_out, dq_out, sems):
+    step = dp.shape[0] // 8
+    copies = [pltpu.make_async_copy(dq, dq_out, sems.at[8])]
+    for k in range(8):
+        part = pl.ds(k * step, step)
+        copies.append(pltpu.make_async_copy(dp.at[part], dp_out.at[part], sems.at[k]))
+    for cp in copies:
+        cp.start()
+    for cp in copies:
+        cp.wait()
+
+
+def run_hand_over(dp, dq):
+    anywhere = pl.BlockSpec(memory_space=pl.ANY)
+    return pl.pallas_call(
+        hand_over,
+        out_shape=(
+            jax.ShapeDtypeStruct(dp.shape, dp.dtype), jax.ShapeDtypeStruct(dq.shape, dq.dtype)
+        ),
+        in_specs=[anywhere] * 2,
+        out_specs=(anywhere,) * 2,
+        scratch_shapes=[pltpu.SemaphoreType.DMA((9,))],
+        name="hand_over",
+    )(dp, dq)
 
 
 def local(rows, cols, queries, prototypes, potential, weights, capacity, cotangent):
@@ -543,7 +605,8 @@
         capacity.reshape(tiles, 1, width), cotangent,
     )
     if fused:
-        return (dq, dp.reshape(slots, feats))
+        grad_protos, grad_queries = run_hand_over(dp.reshape(slots, feats), dq)
+        return (grad_queries, grad_protos)
     whole = lax.psum(dp, "rows")
     whole = whole.transpose(0, 2, 1).reshape(slots, feats)
     return (dq, unit_back(whole, *unit_rows(prototypes)))

time: 127 us -> 249 us (1.96)
  Pallas kernels: 120 us -> 249 us
  local copies, waits for them, and re-layouts: 6.04 us -> 0 us
    pallas_call x0 -> x1, Pallas kernels: none -> 132 us  [run_hand_over(): pl.pallas_call(hand_over, out_shape=(jax.ShapeDtypeStruct(dp.shape, dp.dt...]
    unnamed x2 -> x0, local copies, waits for them, and re-layouts: 6.04 us -> none
    pallas_call x1, Pallas kernels: 120 us -> 116 us  [run_main(): pl.pallas_call(functools.partial(main_kernel, rows, cols, fused), out_sha...]
where the time goes in v4:
time: 249 us
  Pallas kernels  249 us (100%)
    pallas_call x1, Pallas kernels, run_hand_over(): pl.pallas_call(hand_over, out_shape=(jax.ShapeDtypeStruct(dp.shape, dp.dt...  132 us
    pallas_call x1, Pallas kernels, run_main(): pl.pallas_call(functools.partial(main_kernel, rows, cols, fused), out_sha...  116 us

profile of v4, /device:TPU:0, one launch (start us, length us, event | category | flops | bytes accessed | tf_op | source)
XLA Modules:
  0.0 249.3 jit_solution(3112201066324578780)
XLA Ops:
  0.6 116.5 %transport_sweeps.1 = (f32[16,512,128]{2,1,0:T(8,128)}, f32[256,128]{1,0:T(8,128)}) custom-call(bf16[512,128]{1,0:T(8,128)(2,1)} %queries_in.1, bf16[16,512,128]{2,1,0:T(8,128)(2,1)} %bitcast.6, f32[16,1,512]{2,1,0:T(1,128)} %bitcast.7, s32[1,512]{1,0:T(1,128)} %bitcast.9, s32[16,1,512]{2,1,0:T(1,128)} %bitcast.8, bf16[512,128]{1,0:T(8,128)(2,1)} %cotangent.1), custom_call_target="tpu_custom_call" | custom-call | tf_op jit(solution)/shard_map/transport_sweeps/pallas_call | solution.py:544
  117.1 132.2 %hand_over.1 = (f32[8192,128]{1,0:T(8,128)}, f32[256,128]{1,0:T(8,128)}) custom-call(f32[8192,128]{1,0:T(8,128)} %bitcast.5, f32[256,128]{1,0:T(8,128)} %get-tuple-element.7.dq), custom_call_target="tpu_custom_call" | custom-call | tf_op jit(solution)/shard_map/hand_over/pallas_call | solution.py:586

commit v5 on v4

--- a/solution.py
+++ b/solution.py
@@ -414,6 +414,16 @@
         cp.start()
         copies.append(cp)
 
+    def queries_done():
+        for cp in copies:
+            cp.wait()
+        begin = pl.ds(pl.multiple_of(c * piece, 16), piece)
+        mine = dqacc[begin, :]
+        for o in range(1, cols):
+            mine = mine + dqbuf[o]
+        unit, length = unit_rows(queries_in[begin, :])
+        dq_out[...] = unit_back(mine, unit, length)
+
     if fused:
         count = len(lanes)
 
@@ -510,20 +520,15 @@
                 copy_z1(k, r, h).wait_send()
                 copy_z2(k, r, h).wait_send()
 
+        queries_done()
         for h in range(count):
             finish(h)
 
     if direct:
         spread_sent(beta, bsend, brecv)
         spread_sent(shift, hsend, hrecv)
-    for cp in copies:
-        cp.wait()
-    begin = pl.ds(pl.multiple_of(c * piece, 16), piece)
-    mine = dqacc[begin, :]
-    for o in range(1, cols):
-        mine = mine + dqbuf[o]
-    unit, length = unit_rows(queries_in[begin, :])
-    dq_out[...] = unit_back(mine, unit, length)
+    if not fused:
+        queries_done()
 
 
 def run_main(rows, cols, fused, *args):
@@ -569,16 +574,30 @@
     )(*args)
 
 
-def hand_over(dp, dq, dp_out, dq_out, sems):
-    step = dp.shape[0] // 8
-    copies = [pltpu.make_async_copy(dq, dq_out, sems.at[8])]
-    for k in range(8):
+def hand_over(dp, dq, dp_out, dq_out, held, heldq, ins, outs):
+    parts = ins.shape[0] - 1
+    step = dp.shape[0] // parts
+    legs = [
+        (
+            pltpu.make_async_copy(dq, heldq, ins.at[parts]),
+            pltpu.make_async_copy(heldq, dq_out, outs.at[parts]),
+        )
+    ]
+    for k in range(parts):
         part = pl.ds(k * step, step)
-        copies.append(pltpu.make_async_copy(dp.at[part], dp_out.at[part], sems.at[k]))
-    for cp in copies:
-        cp.start()
-    for cp in copies:
-        cp.wait()
+        legs.append(
+            (
+                pltpu.make_async_copy(dp.at[part], held.at[part], ins.at[k]),
+                pltpu.make_async_copy(held.at[part], dp_out.at[part], outs.at[k]),
+            )
+        )
+    for come, _ in legs:
+        come.start()
+    for come, go in legs:
+        come.wait()
+        go.start()
+    for _, go in legs:
+        go.wait()
 
 
 def run_hand_over(dp, dq):
@@ -590,7 +609,11 @@
         ),
         in_specs=[anywhere] * 2,
         out_specs=(anywhere,) * 2,
-        scratch_shapes=[pltpu.SemaphoreType.DMA((9,))],
+        scratch_shapes=[
+            pltpu.VMEM(dp.shape, dp.dtype), pltpu.VMEM(dq.shape, dq.dtype),
+            pltpu.SemaphoreType.DMA((9,)), pltpu.SemaphoreType.DMA((9,)),
+        ],
+        compiler_params=pltpu.CompilerParams(vmem_limit_bytes=16 * 1024 * 1024),
         name="hand_over",
     )(dp, dq)
 

time: 249 us -> 123 us (0.49)
  Pallas kernels: 249 us -> 119 us
  local copies, waits for them, and re-layouts: 0 us -> 3.08 us
    pallas_call x1, Pallas kernels: 132 us -> 2.62 us  [run_hand_over(): pl.pallas_call(hand_over, out_shape=(jax.ShapeDtypeStruct(dp.shape, dp.dt...]
    unnamed x0 -> x4, local copies, waits for them, and re-layouts: none -> 3.08 us
where the time goes in v5:
time: 123 us
  Pallas kernels  119 us (97%)
  local copies, waits for them, and re-layouts  3.08 us (3%)
    pallas_call x1, Pallas kernels, run_main(): pl.pallas_call(functools.partial(main_kernel, rows, cols, fused), out_sha...  116 us
    unnamed x4, local copies, waits for them, and re-layouts  3.08 us
    pallas_call x1, Pallas kernels, run_hand_over(): pl.pallas_call(hand_over, out_shape=(jax.ShapeDtypeStruct(dp.shape, dp.dt...  2.62 us

profile of v5, /device:TPU:0, one launch (start us, length us, event | category | flops | bytes accessed | tf_op | source)
XLA Modules:
  0.0 122.8 jit_solution(10709211629426898190)
XLA Ops:
  0.6 116.5 %transport_sweeps.1 = (f32[16,512,128]{2,1,0:T(8,128)}, f32[256,128]{1,0:T(8,128)}) custom-call(bf16[512,128]{1,0:T(8,128)(2,1)} %queries_in.1, bf16[16,512,128]{2,1,0:T(8,128)(2,1)} %bitcast.6, f32[16,1,512]{2,1,0:T(1,128)} %bitcast.7, s32[1,512]{1,0:T(1,128)} %bitcast.9, s32[16,1,512]{2,1,0:T(1,128)} %bitcast.8, bf16[512,128]{1,0:T(8,128)(2,1)} %cotangent.1), custom_call_target="tpu_custom_call" | custom-call | tf_op jit(solution)/shard_map/transport_sweeps/pallas_call | solution.py:549
  117.1 0.0 copy-start
  117.1 2.2 %copy-done = f32[16,512,128]{2,1,0:T(8,128)S(1)} copy-done((f32[16,512,128]{2,1,0:T(8,128)S(1)}, f32[16,512,128]{2,1,0:T(8,128)}, u32[]{:S(2)}) %copy-start) | copy-done | bytes 4194328
  119.3 0.0 copy-start.1
  119.3 0.9 copy-done.1
  120.2 2.6 %hand_over.1 = (f32[8192,128]{1,0:T(8,128)}, f32[256,128]{1,0:T(8,128)}) custom-call(f32[8192,128]{1,0:T(8,128)S(1)} %bitcast.5, f32[256,128]{1,0:T(8,128)S(1)} %copy-done.1), custom_call_target="tpu_custom_call" | custom-call | tf_op jit(solution)/shard_map/hand_over/pallas_call | solution.py:605
Async XLA Ops:
  117.1 2.2 %copy-start = (f32[16,512,128]{2,1,0:T(8,128)S(1)}, f32[16,512,128]{2,1,0:T(8,128)}, u32[]{:S(2)}) copy-start(f32[16,512,128]{2,1,0:T(8,128)} %get-tuple-element.6) | copy-start | bytes 12582916
  119.3 0.9 copy-start.1

commit v6 on v5

--- a/solution.py
+++ b/solution.py
@@ -45,16 +45,27 @@
 
 def main_kernel(
     rows, cols, fused, queries_in, protos_in, potential, weights, capacity, cotangent,
-    dp_out, dq_out, qhat, scaled, phat, offset, wgt, left_t,
+    dp_out, dq_out, qhat, scaled, phat, offset, left_t,
     kern, coup, zacc, kacc, share, alpha, cbuf, part, pbuf, beta, gpart, gbuf, shift,
-    invs, dqacc, dqbuf, rbuf,
+    invs, dqacc, dqbuf, rbuf, wpool, mine_q, pooled,
     csend, crecv, psend, precv, bsend, brecv, rsend, rrecv, gsend, grecv, hsend, hrecv,
-    dsend, drecv, *ring,
+    dsend, drecv, wsem, qsem, ssem, *ring,
 ):
     tiles, queries, width = kern.shape
+    pool = 2 if fused else 1
+    held = queries // pool
+    group = rows // pool
     lanes = [slice(k, k + LANES) for k in range(0, width, LANES)]
     r = lax.axis_index("rows")
     c = lax.axis_index("cols")
+
+    low = lax.rem(r // 4, 2) if fused else 0
+    high = r // 8
+    g = high * 4 + lax.rem(r, 4) if fused else r
+    twin = r + (1 - 2 * low) * 4 if fused else r
+
+    def row_of(u):
+        return (u // 4) * 8 + low * 4 + lax.rem(u, 4) if fused else u
 
     barrier = pltpu.get_barrier_semaphore()
     for o in range(1, rows):
@@ -65,44 +76,88 @@
         pl.semaphore_signal(
             barrier, inc=1, device_id=(r, lax.rem(c + o, cols)), device_id_type=MESH
         )
+        if fused:
+            pl.semaphore_signal(
+                barrier, inc=1, device_id=(twin, lax.rem(c + o, cols)), device_id_type=MESH
+            )
+    pl.semaphore_wait(barrier, rows - 1 + (cols - 1) * pool)
 
     zacc[...] = jnp.zeros_like(zacc)
     kacc[...] = jnp.zeros_like(kacc)
     dqacc[...] = jnp.zeros_like(dqacc)
     log2e = 1.0 / (TEMPER * math.log(2.0))
-    step = min(queries, 256)
+    step = min(held, 256)
     offset[...] = jnp.log2(capacity[...].astype(jnp.float32)) - potential[...] * log2e
     feats = qhat.shape[1]
-    wgt[...] = jnp.broadcast_to(weights[...].astype(jnp.float32), (feats, queries)).T
-    unit, _ = unit_rows(queries_in[...])
-    qhat[...] = unit
-    left_t[0] = unit.astype(jnp.float32).T.astype(jnp.bfloat16)
-    unit = (cotangent[...].astype(jnp.float32) / wgt[...]).astype(jnp.bfloat16)
-    scaled[...] = unit
-    left_t[1] = unit.astype(jnp.float32).T.astype(jnp.bfloat16)
-
-    def first(t, carry):
-        proto, _ = unit_rows(protos_in[t])
-        phat[t] = proto
-        base = offset[t]
-        for q in range(0, queries, step):
-            qs = slice(q, q + step)
-            k = jnp.exp2(nt_dot(qhat[qs], proto) * log2e + base)
-            g = nt_dot(scaled[qs], proto)
-            kern[t, qs, :] = k
-            coup[t, qs, :] = g
-            kg = k * g
-            zsum = k[:, lanes[0]]
-            gsum = kg[:, lanes[0]]
-            for l in lanes[1:]:
-                zsum = zsum + k[:, l]
-                gsum = gsum + kg[:, l]
-            zacc[qs, :] += zsum
-            kacc[qs, :] += gsum
-        return carry
-
-    lax.fori_loop(0, tiles, first, 0)
-    pl.semaphore_wait(barrier, rows - 1 + cols - 1)
+    wide_w = weights[...].astype(jnp.float32)
+    own_unit, _ = unit_rows(queries_in[...])
+    tall_w = jnp.broadcast_to(wide_w, (feats, held)).T
+    own_scaled = (cotangent[...].astype(jnp.float32) / tall_w).astype(jnp.bfloat16)
+    wpool[low] = wide_w
+    gather = []
+    if fused:
+        mine_q[...] = jnp.where(c == 0, own_unit.astype(jnp.float32), own_scaled.astype(jnp.float32))
+        gather = [
+            push(wpool.at[low], wpool.at[low], wsem.at[0], wsem.at[1], (twin, c)),
+            push(mine_q, pooled.at[c], qsem.at[0], qsem.at[1], (twin, c)),
+        ]
+        for cp in gather:
+            cp.start()
+
+    def place(half):
+        return pl.ds(pl.multiple_of(half * held, held), held)
+
+    qhat[place(low), :] = own_unit
+    scaled[place(low), :] = own_scaled
+
+    def first(half, fresh):
+        def each(t, carry):
+            if fresh:
+                proto, _ = unit_rows(protos_in[row_of(t)])
+                phat[t] = proto
+            else:
+                proto = phat[t]
+            base = offset[row_of(t)]
+            for q in range(0, held, step):
+                qs = pl.ds(pl.multiple_of(half * held + q, step), step)
+                k = jnp.exp2(nt_dot(qhat[qs, :], proto) * log2e + base)
+                grad = nt_dot(scaled[qs, :], proto)
+                kern[t, qs, :] = k
+                coup[t, qs, :] = grad
+                kg = k * grad
+                zsum = k[:, lanes[0]]
+                gsum = kg[:, lanes[0]]
+                for l in lanes[1:]:
+                    zsum = zsum + k[:, l]
+                    gsum = gsum + kg[:, l]
+                zacc[qs, :] += zsum
+                kacc[qs, :] += gsum
+            return carry
+
+        lax.fori_loop(0, tiles, each, 0)
+
+    first(low, True)
+    if fused:
+        gather[1].wait()
+        swap = push(pooled.at[c], pooled.at[c], ssem.at[0], ssem.at[1], (r, 1 - c))
+        swap.start()
+        swap.wait_send()
+        other = push(pooled.at[1 - c], pooled.at[1 - c], ssem.at[0], ssem.at[1], (r, 1 - c))
+        other.wait_recv()
+        gather[0].wait()
+        qhat[place(1 - low), :] = pooled[0].astype(jnp.bfloat16)
+        scaled[place(1 - low), :] = pooled[1].astype(jnp.bfloat16)
+        first(1 - low, False)
+    left_t[0] = qhat[...].astype(jnp.float32).T.astype(jnp.bfloat16)
+    left_t[1] = scaled[...].astype(jnp.float32).T.astype(jnp.bfloat16)
+
+    def mates():
+        for d in range(pool):
+            for o in range(cols):
+                if d + o > 0:
+                    there = twin if d else r
+                    half = 1 - low if d else low
+                    yield d * cols + o, half, there, lax.rem(c + o, cols)
 
     def tall(row):
         return jnp.broadcast_to(row, (LANES, queries)).T
@@ -112,27 +167,25 @@
 
     def over_cols(buf, send, recv):
         copies = []
-        for o in range(1, cols):
-            cp = push(
-                buf.at[0], buf.at[o], send.at[o], recv.at[o], (r, lax.rem(c + o, cols))
-            )
+        for o, _, there, col in mates():
+            cp = push(buf.at[0], buf.at[o], send.at[o], recv.at[o], (there, col))
             cp.start()
             copies.append(cp)
         for cp in copies:
             cp.wait()
         total = buf[0]
-        for o in range(1, cols):
+        for o in range(1, cols * pool):
             total = total + buf[o]
         return total
 
     cbuf[0, 0:1] = flat(zacc)
     cbuf[0, 1:2] = flat(kacc)
     total = over_cols(cbuf, csend, crecv)
-    w = weights[...].astype(jnp.float32)
+    w = jnp.concatenate([wpool[k] for k in range(pool)], axis=1)
     srate = w / total[0:1]
     share[...] = tall(srate)
     alpha[...] = tall(srate * total[1:2] / w)
-    direct = tiles == rows
+    direct = tiles == group
 
     def swept(body, part_ref, buf, send, recv):
         if not direct:
@@ -141,22 +194,22 @@
             return
 
         def each(o, carry):
-            t = lax.rem(r + o, rows)
+            t = lax.rem(g + o, group)
             body(t)
 
-            @pl.when(o < rows)
+            @pl.when(o < group)
             def _():
-                push(part_ref.at[t], buf.at[o], send.at[o], recv.at[o], (t, c)).start()
-
-            return carry
-
-        lax.fori_loop(1, rows + 1, each, 0)
+                push(part_ref.at[t], buf.at[o], send.at[o], recv.at[o], (row_of(t), c)).start()
+
+            return carry
+
+        lax.fori_loop(1, group + 1, each, 0)
 
         def done(o, carry):
-            push(part_ref.at[r], buf.at[o], send.at[o], recv.at[o], (lax.rem(r + o, rows), c)).wait()
-            return carry
-
-        lax.fori_loop(1, rows, done, 0)
+            push(part_ref.at[g], buf.at[o], send.at[o], recv.at[o], (row_of(lax.rem(g + o, group)), c)).wait()
+            return carry
+
+        lax.fori_loop(1, group, done, 0)
 
     def second(t):
         for l in lanes:
@@ -203,73 +256,73 @@
 
     def spread_start(buf, send, recv):
         def each(o, carry):
-            peer = lax.rem(r + o, rows)
+            peer = lax.rem(g + o, group)
 
             def go():
-                push(buf.at[r], buf.at[r], send.at[o], recv.at[o], (peer, c)).start()
-
-            if tiles == rows:
+                push(buf.at[g], buf.at[g], send.at[o], recv.at[o], (row_of(peer), c)).start()
+
+            if tiles == group:
                 go()
             else:
-                pl.when(r < tiles)(go)
-            return carry
-
-        lax.fori_loop(1, rows, each, 0)
+                pl.when(g < tiles)(go)
+            return carry
+
+        lax.fori_loop(1, group, each, 0)
 
     def spread_got(buf, send, recv, t):
-        o = lax.rem(r + rows - t, rows)
+        o = lax.rem(g + group - t, group)
 
         @pl.when(o > 0)
         def _():
-            push(buf.at[t], buf.at[t], send.at[o], recv.at[o], (t, c)).wait_recv()
+            push(buf.at[t], buf.at[t], send.at[o], recv.at[o], (row_of(t), c)).wait_recv()
 
     def spread_sent(buf, send, recv):
         def done(o, carry):
             push(
-                buf.at[r], buf.at[r], send.at[o], recv.at[o], (lax.rem(r + o, rows), c)
+                buf.at[g], buf.at[g], send.at[o], recv.at[o], (row_of(lax.rem(g + o, group)), c)
             ).wait_send()
             return carry
 
-        lax.fori_loop(1, rows, done, 0)
+        lax.fori_loop(1, group, done, 0)
 
     def spread_wait(buf, send, recv):
         def done(o, carry):
-            origin = lax.rem(r + rows - o, rows)
-            peer = lax.rem(r + o, rows)
+            origin = lax.rem(g + group - o, group)
+            peer = lax.rem(g + o, group)
 
             def sent():
-                push(buf.at[r], buf.at[r], send.at[o], recv.at[o], (peer, c)).wait_send()
+                push(buf.at[g], buf.at[g], send.at[o], recv.at[o], (row_of(peer), c)).wait_send()
 
             def got():
                 push(
-                    buf.at[origin], buf.at[origin], send.at[o], recv.at[o], (peer, c)
+                    buf.at[origin], buf.at[origin], send.at[o], recv.at[o], (row_of(peer), c)
                 ).wait_recv()
 
-            if tiles == rows:
+            if tiles == group:
                 sent()
                 got()
             else:
-                pl.when(r < tiles)(sent)
+                pl.when(g < tiles)(sent)
                 pl.when(origin < tiles)(got)
             return carry
 
-        lax.fori_loop(1, rows, done, 0)
+        lax.fori_loop(1, group, done, 0)
 
     def own(body):
-        if tiles == rows:
+        if tiles == group:
             body()
         else:
-            pl.when(r < tiles)(body)
+            pl.when(g < tiles)(body)
 
     swept(second, part, pbuf, psend, precv)
 
     def first_beta():
-        both = part[r]
-        for o in range(1, rows):
+        both = part[g]
+        for o in range(1, group):
             both = both + pbuf[o]
         inv = 1.0 / both[0:1]
         invs[...] = inv
-        beta[r] = both[1:2] * inv
+        beta[g] = both[1:2] * inv
 
     own(first_beta)
     zacc[...] = jnp.zeros_like(zacc)
@@ -280,7 +333,7 @@
     def third(o, carry):
         t = o
         if direct:
-            t = lax.rem(r + rows - o, rows)
+            t = lax.rem(g + group - o, group)
             spread_got(beta, bsend, brecv, t)
         acc = zacc[...]
         for l in lanes:
@@ -301,10 +354,10 @@
     swept(fourth, gpart, gbuf, gsend, grecv)
 
     def second_beta():
-        tot = gpart[r]
-        for o in range(1, rows):
+        tot = gpart[g]
+        for o in range(1, group):
             tot = tot + gbuf[o]
-        shift[r] = beta[r] + tot * invs[...]
+        shift[g] = beta[g] + tot * invs[...]
 
     own(second_beta)
     spread_start(shift, hsend, hrecv)
@@ -350,6 +403,7 @@
         lax.fori_loop(0, tiles, plain, 0)
     else:
         depth = rows // 4
+        near = depth // 2
         z = r // 4
         even = lax.rem(c, 2) == 0
         wa = jnp.where(even, 1, 2)
@@ -359,6 +413,9 @@
         peer_a = r + (1 - 2 * a) * wa
         peer_b = r + (1 - 2 * b) * wb
 
+        def ahead_near(k):
+            return lax.rem(high + 1 + k, near)
+
         def spot(zz, av, bv):
             return zz * 4 + av * wa + bv * wb
 
@@ -374,11 +431,11 @@
         def copy_z1(k, t, h):
             return push(
                 dp.at[t, h], rs3.at[k, h], s3s.at[k, h], s3r.at[k, h],
-                (spot(ahead(k), a, b), c),
+                (row_of(spot(ahead_near(k), a, b)), c),
             )
 
         def away(i):
-            return spot(ahead(lax.rem(i, depth)), 1 - a, jnp.where(i < depth, 1 - b, b))
+            return spot(ahead_near(lax.rem(i, near)), 1 - a, jnp.where(i < near, 1 - b, b))
 
         def leave(i, carry):
             t = away(i)
@@ -386,30 +443,33 @@
             copy_a1(i, t, 0).start()
             return carry
 
-        lax.fori_loop(0, 2 * depth, leave, 0)
+        lax.fori_loop(0, 2 * near, leave, 0)
 
         def leave_piece(h):
             def each(i, carry):
                 copy_a1(i, away(i), h).start()
                 return carry
 
-            lax.fori_loop(0, 2 * depth, each, 0)
+            lax.fori_loop(0, 2 * near, each, 0)
 
         leave_piece(1)
 
         def stay(i, carry):
-            fifth(spot(ahead(lax.rem(i, depth)), a, jnp.where(i < depth, 1 - b, b)))
-            return carry
-
-        lax.fori_loop(0, 2 * depth, stay, 0)
-
-    piece = queries // cols
+            fifth(spot(ahead_near(lax.rem(i, near)), a, jnp.where(i < near, 1 - b, b)))
+            return carry
+
+        lax.fori_loop(0, 2 * near, stay, 0)
+
+    piece = held // cols
+
+    def piece_at(half, col):
+        return pl.ds(pl.multiple_of(half * held + col * piece, piece), piece)
+
     copies = []
-    for o in range(1, cols):
-        peer = lax.rem(c + o, cols)
+    for o, half, there, col in mates():
         cp = push(
-            dqacc.at[pl.ds(pl.multiple_of(peer * piece, 8), piece)],
-            dqbuf.at[o], dsend.at[o], drecv.at[o], (r, peer),
+            dqacc.at[piece_at(half, col)],
+            dqbuf.at[o], dsend.at[o], drecv.at[o], (there, col),
         )
         cp.start()
         copies.append(cp)
@@ -417,11 +477,10 @@
     def queries_done():
         for cp in copies:
             cp.wait()
-        begin = pl.ds(pl.multiple_of(c * piece, 16), piece)
-        mine = dqacc[begin, :]
-        for o in range(1, cols):
+        mine = dqacc[piece_at(low, c), :]
+        for o in range(1, cols * pool):
             mine = mine + dqbuf[o]
-        unit, length = unit_rows(queries_in[begin, :])
+        unit, length = unit_rows(queries_in[piece_at(0, c), :])
         dq_out[...] = unit_back(mine, unit, length)
 
     if fused:
@@ -429,28 +488,28 @@
 
         def hop_b(h):
             def each(k, carry):
-                t = spot(ahead(k), a, 1 - b)
+                t = spot(ahead_near(k), a, 1 - b)
                 copy_a1(k, t, h).wait_recv()
                 dp[t, h] += rs1[k, h]
                 copy_b1(k, t, h).start()
                 return carry
 
-            lax.fori_loop(0, depth, each, 0)
+            lax.fori_loop(0, near, each, 0)
 
         def hop_z(h):
             def each(k, carry):
-                t = spot(ahead(k), a, b)
-                copy_a1(depth + k, t, h).wait_recv()
+                t = spot(ahead_near(k), a, b)
+                copy_a1(near + k, t, h).wait_recv()
                 copy_b1(k, t, h).wait_recv()
-                dp[t, h] += rs1[depth + k, h] + rs2[k, h]
-
-                @pl.when(k < depth - 1)
+                dp[t, h] += rs1[near + k, h] + rs2[k, h]
+
+                @pl.when(k < near - 1)
                 def _():
                     copy_z1(k, t, h).start()
 
                 return carry
 
-            lax.fori_loop(0, depth, each, 0)
+            lax.fori_loop(0, near, each, 0)
 
         def block(t, h):
             return dp_out.at[t, pl.ds(h * LANES, LANES)]
@@ -471,9 +530,9 @@
             return lax.rem(z + depth - m, depth)
 
         def settle(h):
-            total = dp[r, h]
-            for k in range(depth - 1):
-                copy_z1(k, r, h).wait_recv()
+            total = dp[g, h]
+            for k in range(near - 1):
+                copy_z1(k, g, h).wait_recv()
                 total = total + rs3[k, h]
             rows_h = pl.ds(h * LANES, LANES)
             unit, length = unit_rows(protos_in[r, rows_h])
@@ -510,14 +569,17 @@
             for m in range(depth):
                 copy_a2(2 * m, spot(behind(m), 1 - a, b), h).wait_recv()
                 copy_a2(2 * m + 1, spot(behind(m), 1 - a, 1 - b), h).wait_recv()
+            for k in range(2 * near):
+                copy_a1(k, g, h).wait_send()
+            for k in range(near):
+                copy_b1(k, g, h).wait_send()
+            for k in range(near - 1):
+                copy_z1(k, g, h).wait_send()
             for k in range(2 * depth):
-                copy_a1(k, r, h).wait_send()
                 copy_a2(k, r, h).wait_send()
             for k in range(depth):
-                copy_b1(k, r, h).wait_send()
                 copy_b2(k, r, h).wait_send()
             for k in range(depth - 1):
-                copy_z1(k, r, h).wait_send()
                 copy_z2(k, r, h).wait_send()
 
         queries_done()
@@ -532,41 +594,46 @@
 
 
 def run_main(rows, cols, fused, *args):
-    queries, feats = args[0].shape
-    tiles, width, _ = args[1].shape
+    held, feats = args[0].shape
+    total, width, _ = args[1].shape
+    pool = 2 if fused else 1
+    queries, tiles, group = held * pool, total // pool, rows // pool
+    mates = cols * pool
     bf16 = jnp.bfloat16
     f32 = jnp.float32
     vec = lambda *s: pltpu.VMEM(s, f32)
-    sems_r = [pltpu.SemaphoreType.DMA((rows,))] * 2
-    sems_c = [pltpu.SemaphoreType.DMA((cols,))] * 2
+    sems_r = [pltpu.SemaphoreType.DMA((group,))] * 2
+    sems_c = [pltpu.SemaphoreType.DMA((mates,))] * 2
     ring = []
     if fused:
         depth = rows // 4
+        near = depth // 2
         cuts = width // LANES
-        ring = [vec(n, cuts, feats, LANES) for n in (tiles, 2 * depth, depth, depth)]
-        for count in (2, 1, 1, 2, 1, 1):
-            ring += [pltpu.SemaphoreType.DMA((count * depth, cuts))] * 2
+        ring = [vec(n, cuts, feats, LANES) for n in (tiles, 2 * near, near, near)]
+        for count in (2 * near, near, near, 2 * depth, depth, depth):
+            ring += [pltpu.SemaphoreType.DMA((count, cuts))] * 2
     return pl.pallas_call(
         functools.partial(main_kernel, rows, cols, fused),
         out_shape=(
-            jax.ShapeDtypeStruct((tiles, width, feats) if fused else (tiles, feats, width), f32),
-            jax.ShapeDtypeStruct((queries // cols, feats), f32),
+            jax.ShapeDtypeStruct((total, width, feats) if fused else (total, feats, width), f32),
+            jax.ShapeDtypeStruct((held // cols, feats), f32),
         ),
         in_specs=[pl.BlockSpec(memory_space=pltpu.VMEM)] * 6,
         out_specs=(pl.BlockSpec(memory_space=pltpu.VMEM),) * 2,
         scratch_shapes=[
             pltpu.VMEM((queries, feats), bf16), pltpu.VMEM((queries, feats), bf16),
-            pltpu.VMEM((tiles, width, feats), bf16), vec(tiles, 1, width),
-            vec(queries, LANES), pltpu.VMEM((2, feats, queries), bf16),
+            pltpu.VMEM((tiles, width, feats), bf16), vec(total, 1, width),
+            pltpu.VMEM((2, feats, queries), bf16),
             vec(tiles, queries, width), vec(tiles, queries, width),
             vec(queries, LANES), vec(queries, LANES), vec(queries, LANES), vec(queries, LANES),
-            vec(cols, 2, queries),
-            vec(tiles, 2, width), vec(rows, 2, width), vec(tiles, 1, width),
-            vec(tiles, 1, width), vec(rows, 1, width), vec(tiles, 1, width),
+            vec(mates, 2, queries),
+            vec(tiles, 2, width), vec(group, 2, width), vec(tiles, 1, width),
+            vec(tiles, 1, width), vec(group, 1, width), vec(tiles, 1, width),
             vec(1, width), vec(queries, feats),
-            vec(cols, queries // cols, feats), vec(cols, 1, queries),
+            vec(mates, held // cols, feats), vec(mates, 1, queries),
+            vec(pool, 1, held), vec(held, feats), vec(2, held, feats),
         ]
-        + sems_c + sems_r + sems_r + sems_c + sems_r + sems_r + sems_c + ring,
+        + sems_c + sems_r + sems_r + sems_c + sems_r + sems_r + sems_c + [pltpu.SemaphoreType.DMA((2,))] * 3 + ring,
         compiler_params=pltpu.CompilerParams(
             collective_id=0, has_side_effects=True, vmem_limit_bytes=56 * 1024 * 1024
         ),
@@ -613,7 +680,7 @@
             pltpu.VMEM(dp.shape, dp.dtype), pltpu.VMEM(dq.shape, dq.dtype),
             pltpu.SemaphoreType.DMA((9,)), pltpu.SemaphoreType.DMA((9,)),
         ],
-        compiler_params=pltpu.CompilerParams(vmem_limit_bytes=16 * 1024 * 1024),
+        compiler_params=pltpu.CompilerParams(vmem_limit_bytes=56 * 1024 * 1024),
         name="hand_over",
     )(dp, dq)
 
@@ -621,7 +688,7 @@
 def local(rows, cols, queries, prototypes, potential, weights, capacity, cotangent):
     slots, feats = prototypes.shape
     width, tiles = tiles_of(slots, rows)
-    fused = tiles == rows and rows % 4 == 0
+    fused = tiles == rows and rows % 8 == 0 and cols == 2
     dp, dq = run_main(
         rows, cols, fused, queries, prototypes.reshape(tiles, width, feats),
         potential.reshape(tiles, 1, width), weights.reshape(1, -1),

time: 123 us -> 117 us (0.951)
  local copies, waits for them, and re-layouts: 3.08 us -> 0 us
  Pallas kernels: 119 us -> 116 us
    pallas_call x1, Pallas kernels: 116 us -> 112 us  [run_main(): pl.pallas_call(functools.partial(main_kernel, rows, cols, fused), out_sha...]
    unnamed x4 -> x0, local copies, waits for them, and re-layouts: 3.08 us -> none
where the time goes in v6:
time: 117 us
  Pallas kernels  116 us (99%)
    pallas_call x1, Pallas kernels, run_main(): pl.pallas_call(functools.partial(main_kernel, rows, cols, fused), out_sha...  112 us
    pallas_call x1, Pallas kernels, run_hand_over(): pl.pallas_call(hand_over, out_shape=(jax.ShapeDtypeStruct(dp.shape, dp.dt...  3.81 us

profile of v6, /device:TPU:0, one launch (start us, length us, event | category | flops | bytes accessed | tf_op | source)
XLA Modules:
  0.0 116.6 jit_solution(3827560416906227335)
XLA Ops:
  0.6 112.2 %transport_sweeps.1 = (f32[16,512,128]{2,1,0:T(8,128)}, f32[256,128]{1,0:T(8,128)}) custom-call(bf16[512,128]{1,0:T(8,128)(2,1)} %queries_in.1, bf16[16,512,128]{2,1,0:T(8,128)(2,1)} %bitcast.6, f32[16,1,512]{2,1,0:T(1,128)} %bitcast.7, s32[1,512]{1,0:T(1,128)} %bitcast.9, s32[16,1,512]{2,1,0:T(1,128)} %bitcast.8, bf16[512,128]{1,0:T(8,128)(2,1)} %cotangent.1), custom_call_target="tpu_custom_call" | custom-call | tf_op jit(solution)/shard_map/transport_sweeps/pallas_call | solution.py:615
  112.8 3.8 %hand_over.1 = (f32[8192,128]{1,0:T(8,128)}, f32[256,128]{1,0:T(8,128)}) custom-call(f32[8192,128]{1,0:T(8,128)} %bitcast.5, f32[256,128]{1,0:T(8,128)} %get-tuple-element.7.dq), custom_call_target="tpu_custom_call" | custom-call | tf_op jit(solution)/shard_map/hand_over/pallas_call | solution.py:672
